TPU v7x, 32 devices: a whole 2x2x4 slice. The times are simulated.
32 devices in a mesh: lat: 4 (over x, core), lon: 8 (over z, y).
Axes of the slice: x: 2, y: 2, z: 4, core: 2. Of those that a mesh axis runs over, the one named last changes fastest.
Arguments:
- node_latents: bfloat16 [8192, 512], P(('lat', 'lon')), may hold values from -6 to 6
- edge_latents: bfloat16 [65536, 512], P(('lat', 'lon')), may hold values from -6 to 6
- edge_count: int32 [32], P(('lat', 'lon')), may hold values from 256 to 2048, as said below
- receiver: int32 [65536], P(('lat', 'lon')), may hold values from 0 to 255, as said below
- sender: int32 [65536], P(('lat', 'lon')), may hold values from 0 to 447, as said below
- halo_send: int32 [32, 4, 32], P(('lat', 'lon')), may hold values from 0 to 255
- far_send: int32 [32, 32, 2], P(('lat', 'lon')), may hold values from 0 to 255
- edge_weight_in: bfloat16 [1536, 512], replicated, may hold values from -0.15625 to 0.15625
- edge_bias: float32 [512], replicated, may hold values from -3 to 3
- edge_weight_out: bfloat16 [512, 512], replicated, may hold values from -0.25 to 0.25
- edge_gain: float32 [512], replicated, may hold values from 0.25 to 1.75
- node_weight_in: bfloat16 [1024, 512], replicated, may hold values from -0.1875 to 0.1875
- node_bias: float32 [512], replicated, may hold values from -3 to 3
- node_weight_out: bfloat16 [512, 512], replicated, may hold values from -0.25 to 0.25
- node_gain: float32 [512], replicated, may hold values from 0.25 to 1.75
- cot_nodes: bfloat16 [8192, 512], P(('lat', 'lon')), may hold values from -6 to 6
- cot_edges: bfloat16 [65536, 512], P(('lat', 'lon')), may hold values from -6 to 6
Outputs:
- node_out: bfloat16 [8192, 512], P(('lat', 'lon'))
- edge_out: bfloat16 [65536, 512], P(('lat', 'lon'))
- grad_nodes: bfloat16 [8192, 512], P(('lat', 'lon'))
- grad_edges: bfloat16 [65536, 512], P(('lat', 'lon'))
- grad_edge_weight_in: float32 [1536, 512], replicated
- grad_edge_bias: float32 [512], replicated
- grad_edge_weight_out: float32 [512, 512], replicated
- grad_edge_gain: float32 [512], replicated
- grad_node_weight_in: float32 [1024, 512], replicated
- grad_node_bias: float32 [512], replicated
- grad_node_weight_out: float32 [512, 512], replicated
- grad_node_gain: float32 [512], replicated
Inputs may be any that keep to these rules, and one draw needn't show every extreme that they name: `edge_count`: edge slots of a device past its count are padding; some device has all 2048 slots live in every draw. `receiver`: nondecreasing within each device's 2048 edge slots. `sender`: rows below 256 are the device's own nodes, the next 128 the four neighbours' halo rows, the rest the 2 rows from each peer in device order; halo rows from a band that does not exist are never named.
All inputs are finite; a program needn't handle non-finite values.
Results may differ from a plain program's by a relative error of at most 0.017.
Values may be sent and summed in bfloat16 or wider, within the bound.
No kernel may reach another device: no remote copies, remote signals or barrier semaphores. Data moves between devices by JAX's collectives and lax.ppermute only.
A program may use at most 128 MiB of HBM per device.

v0:
```python
from functools import partial

import jax
import jax.numpy as jnp
from jax import lax
from jax.sharding import PartitionSpec as P

EPSILON = 1e-05


def padded(array, sides, width, wrap):
    for axis, dim in sides:
        size, length = (lax.axis_size(axis), array.shape[dim])
        up = [(i, (i + 1) % size) for i in range(size if wrap else size - 1)]
        down = [(j, i) for i, j in up]
        last = lax.slice_in_dim(array, length - width, length, axis=dim)
        first = lax.slice_in_dim(array, 0, width, axis=dim)
        before = lax.ppermute(last, axis, up)
        after = lax.ppermute(first, axis, down)
        array = jnp.concatenate([before, array, after], axis=dim)
    return array


def layer_norm(values, gain_out):
    row_mean = jnp.mean(values, axis=-1, keepdims=True)
    centered = values - row_mean
    variance = jnp.mean(centered * centered, axis=-1, keepdims=True)
    return centered * lax.rsqrt(variance + EPSILON) * gain_out


def edge_update(params, edge_rows, sender_rows, receiver_rows, live_mask):
    weight_in, bias_in, weight_out, gain_out = params
    joined = jnp.concatenate([edge_rows, sender_rows, receiver_rows], axis=1)
    first_layer = jnp.dot(joined, weight_in, preferred_element_type=jnp.float32) + bias_in
    active = jax.nn.silu(first_layer).astype(jnp.bfloat16)
    second = jnp.dot(active, weight_out, preferred_element_type=jnp.float32)
    message = layer_norm(second, gain_out) * live_mask[:, None]
    updated = (edge_rows.astype(jnp.float32) + message).astype(jnp.bfloat16)
    return (updated, message)


def node_update(params, node_rows, gathered):
    weight_in, bias_in, weight_out, gain_out = params
    joined = jnp.concatenate([node_rows, gathered], axis=1)
    first_layer = jnp.dot(joined, weight_in, preferred_element_type=jnp.float32) + bias_in
    active = jax.nn.silu(first_layer).astype(jnp.bfloat16)
    second = jnp.dot(active, weight_out, preferred_element_type=jnp.float32)
    return (node_rows.astype(jnp.float32) + layer_norm(second, gain_out)).astype(jnp.bfloat16)


def shards(
    node_latents,
    edge_latents,
    edge_count,
    receiver,
    sender,
    halo_send,
    far_send,
    edge_weight_in,
    edge_bias,
    edge_weight_out,
    edge_gain,
    node_weight_in,
    node_bias,
    node_weight_out,
    node_gain,
    cot_nodes,
    cot_edges,
):
    node_rows, feature_width = node_latents.shape
    edge_rows = edge_latents.shape[0]
    border = halo_send.shape[2]
    peer_count = far_send.shape[1]
    capacity = far_send.shape[2]
    rim_lists = halo_send[0]
    far_lists = far_send[0].reshape(-1)
    lat_outgoing = jnp.concatenate([node_latents[rim_lists[0]], node_latents[rim_lists[1]]], axis=0)
    lat_rims = padded(lat_outgoing, (("lat", 0),), border, False)
    lon_outgoing = jnp.concatenate([node_latents[rim_lists[2]], node_latents[rim_lists[3]]], axis=0)
    lon_rims = padded(lon_outgoing, (("lon", 0),), border, True)
    far_outgoing = node_latents[far_lists].reshape(peer_count, capacity, feature_width)
    incoming = lax.all_to_all(far_outgoing, ("lat", "lon"), split_axis=0, concat_axis=0, tiled=True)
    sender_table = jnp.concatenate(
        [
            node_latents,
            lat_rims[:border],
            lat_rims[3 * border :],
            lon_rims[:border],
            lon_rims[3 * border :],
            incoming.reshape(peer_count * capacity, feature_width),
        ],
        axis=0,
    )
    live_mask = (lax.iota(jnp.int32, edge_rows) < edge_count[0]).astype(jnp.float32)
    sent_rows = sender_table[sender]
    received_rows = node_latents[receiver]
    edge_params = (edge_weight_in, edge_bias, edge_weight_out, edge_gain)
    node_params = (node_weight_in, node_bias, node_weight_out, node_gain)
    (new_edges, message), edge_back = jax.vjp(
        partial(edge_update, live_mask=live_mask),
        edge_params,
        edge_latents,
        sent_rows,
        received_rows,
    )
    gathered = jax.ops.segment_sum(message, receiver, node_rows, indices_are_sorted=True).astype(
        jnp.bfloat16
    )
    new_nodes, node_back = jax.vjp(node_update, node_params, node_latents, gathered)
    node_grads, from_node, from_gathered = node_back(cot_nodes)
    edge_grads, edge_grad, from_send, from_receive = edge_back(
        (cot_edges, from_gathered.astype(jnp.float32)[receiver])
    )
    totals = from_node.astype(jnp.float32) + jax.ops.segment_sum(
        from_receive.astype(jnp.float32), receiver, node_rows, indices_are_sorted=True
    )
    slot_grads = jax.ops.segment_sum(
        from_send.astype(jnp.float32), sender, node_rows + 4 * border + peer_count * capacity
    )
    totals = totals + slot_grads[:node_rows]
    lat_back = padded(
        slot_grads[node_rows : node_rows + 2 * border].astype(jnp.bfloat16),
        (("lat", 0),),
        border,
        False,
    ).astype(jnp.float32)
    lon_back = padded(
        slot_grads[node_rows + 2 * border : node_rows + 4 * border].astype(jnp.bfloat16),
        (("lon", 0),),
        border,
        True,
    ).astype(jnp.float32)
    totals = (
        totals.at[rim_lists[0]].add(lat_back[:border]).at[rim_lists[1]].add(lat_back[3 * border :])
    )
    totals = (
        totals.at[rim_lists[2]].add(lon_back[:border]).at[rim_lists[3]].add(lon_back[3 * border :])
    )
    far_back = slot_grads[node_rows + 4 * border :].reshape(peer_count, capacity, feature_width)
    returned = lax.all_to_all(
        far_back.astype(jnp.bfloat16), ("lat", "lon"), split_axis=0, concat_axis=0, tiled=True
    ).astype(far_back.dtype)
    totals = totals.at[far_lists].add(returned.reshape(peer_count * capacity, feature_width))
    grad_nodes = totals.astype(jnp.bfloat16)
    every_grad = tuple((grad.astype(jnp.float32) for grad in tuple(edge_grads) + tuple(node_grads)))
    summed = lax.psum(every_grad, ("lat", "lon"))
    return (
        new_nodes,
        new_edges,
        grad_nodes,
        edge_grad,
        summed[0],
        summed[1],
        summed[2],
        summed[3],
        summed[4],
        summed[5],
        summed[6],
        summed[7],
    )


def solution(mesh):
    return jax.shard_map(
        shards,
        mesh=mesh,
        in_specs=(
            P(("lat", "lon"), None),
            P(("lat", "lon"), None),
            P(("lat", "lon")),
            P(("lat", "lon")),
            P(("lat", "lon")),
            P(("lat", "lon"), None, None),
            P(("lat", "lon"), None, None),
            P(),
            P(),
            P(),
            P(),
            P(),
            P(),
            P(),
            P(),
            P(("lat", "lon"), None),
            P(("lat", "lon"), None),
        ),
        out_specs=(
            P(("lat", "lon"), None),
            P(("lat", "lon"), None),
            P(("lat", "lon"), None),
            P(("lat", "lon"), None),
            P(),
            P(),
            P(),
            P(),
            P(),
            P(),
            P(),
            P(),
        ),
        check_vma=False,
    )
```

profile of v0, /device:TPU:0, one launch (start us, length us, event | category | flops | bytes accessed | tf_op | source)
XLA Modules:
  0.0 334.3 jit_solution(4237935056823433590)
XLA Ops:
  8.1 1.6 gather_fusion
  9.7 2.4 collective-permute-start
  12.1 1.6 gather_fusion.1
  13.7 1.3 collective-permute-start.1
  15.1 1.6 gather_fusion.2
  16.7 2.4 collective-permute-start.2
  19.1 1.6 gather_fusion.3
  20.7 3.1 collective-permute-start.3
  24.7 1.7 gather_fusion.4
  27.1 5.8 %all-to-all-start = ((bf16[32,2,512]{2,1,0:T(2,128)(2,1)}), bf16[32,2,512]{2,1,0:T(2,128)(2,1)S(1)}, u32[]{:S(2)}, u32[]{:S(2)}) async-start(bf16[32,2,512]{2,1,0:T(2,128)(2,1)} %reshape.255), calls=%async_computation | async-start | bytes 131072 | tf_op jit(solution)/shard_map/all_to_all | solution.py:82
  34.7 3.2 constant_dynamic-update-slice_fusion.8
  38.5 3.9 %copy.36 = bf16[2048,512]{0,1:T(8,128)(2,1)} copy(bf16[2048,512]{1,0:T(8,128)(2,1)} %param.18) | data formatting | bytes 4194304 | tf_op args[1]
  42.4 9.2 %gather_fusion.6 = bf16[2048,512]{1,0:T(8,128)(2,1)} fusion(bf16[256,512]{1,0:T(8,128)(2,1)S(1)} %copy-done.1, s32[2048]{0:T(1024)S(1)} %fusion.63), kind=kCustom, calls=%fused_computation.6 | custom fusion | bytes 4202496 | tf_op jit(solution)/shard_map/gather | solution.py:96
  51.6 3.9 %copy.37 = bf16[2048,512]{0,1:T(8,128)(2,1)} copy(bf16[2048,512]{1,0:T(8,128)(2,1)} %param.33) | data formatting | bytes 4194304 | tf_op args[16]
  55.7 9.2 %gather_fusion.5 = bf16[2048,512]{1,0:T(8,128)(2,1)} fusion(bf16[448,512]{1,0:T(8,128)(2,1)S(1)} %constant_dynamic-update-slice_fusion, s32[2048]{0:T(1024)S(1)} %fusion.62), kind=kCustom, calls=%fused_computation.5 | custom fusion | bytes 4202496 | tf_op jit(solution)/shard_map/gather | solution.py:95
  64.9 3.3 constant_dynamic-update-slice_fusion.7
  68.2 1.5 constant_dynamic-update-slice_fusion.6
  69.7 5.5 %fusion.84 = f32[2048,512]{1,0:T(8,128)S(1)} fusion(bf16[2048,1536]{1,0:T(8,128)(2,1)} %constant_dynamic-update-slice_fusion.6, bf16[1536,512]{1,0:T(8,128)(2,1)S(1)} %copy-done), kind=kOutput, calls=%fused_computation.158 | convolution fusion | flops 3221225472 | bytes 12058624 | tf_op jit(solution)/shard_map/jvp()/dot_general | solution.py:34
  75.3 1.6 fusion.80
  77.8 2.6 copy-done.7
  80.4 3.9 %add_convert_fusion = (bf16[2048,512]{0,1:T(8,128)(2,1)}, f32[2048,512]{0,1:T(8,128)}) fusion(bf16[2048,512]{0,1:T(8,128)(2,1)S(1)} %copy-done.7, f32[2048]{0:T(1024)S(1)} %fusion.64, f32[512]{0:T(512)S(1)} %copy-done.14, f32[2048]{0:T(1024)S(1)} %fusion.65, f32[2048,512]{0,1:T(8,128)S(1)} %get-tuple-element.67, f32[2048]{0:T(1024)S(1)} %broadcast_multiply_fusion), kind=kLoop, calls=%fused_computation.30 | loop fusion | flops 7340032 | bytes 12609536 | tf_op jit(solution)/shard_map/jvp()/convert_element_type | solution.py:38
  84.3 5.4 %copy.35 = f32[2048,512]{1,0:T(8,128)} copy(f32[2048,512]{0,1:T(8,128)} %get-tuple-element.53) | data formatting | bytes 8388608 | tf_op jit(solution)/shard_map/jvp()/mul | solution.py:37
  89.7 15.2 %scatter_custom_fusion = f32[256,512]{1,0:T(8,128)S(1)} fusion(s32[2048]{0:T(1024)S(1)} %copy-done.15, f32[2048,512]{1,0:T(8,128)} %copy.35, f32[]{:T(128)} %constant.10.clone.1), kind=kCustom, calls=%fused_computation.80 | custom fusion | flops 1048576 | bytes 524800 | tf_op jit(solution)/shard_map/scatter-add | solution.py:106
  105.0 1.7 convolution_add_fusion
  106.7 1.4 fusion.81
  110.8 1.4 fusion.25
  112.6 1.8 fusion.18
  114.5 8.9 %gather_fusion.7 = f32[2048,512]{1,0:T(8,128)} fusion(f32[256,512]{1,0:T(8,128)S(1)} %slice_convert_fusion, s32[2048]{0:T(1024)S(1)} %fusion.63), kind=kCustom, calls=%fused_computation.7 | custom fusion | bytes 8396800 | tf_op jit(solution)/shard_map/gather | solution.py:112
  123.4 5.4 %copy.38 = f32[2048,512]{0,1:T(8,128)} copy(f32[2048,512]{1,0:T(8,128)} %gather_fusion.7) | data formatting | bytes 8388608 | tf_op jit(solution)/shard_map/gather | solution.py:112
  128.8 5.8 %multiply_reduce_fusion = (f32[512]{0:T(512)S(1)}, f32[2048]{0:T(1024)S(1)}) fusion(f32[2048,512]{0,1:T(8,128)} %copy-done.2, f32[2048]{0:T(1024)S(1)} %fusion.65, f32[2048]{0:T(1024)S(1)} %broadcast_multiply_fusion, f32[2048]{0:T(1024)S(1)} %fusion.64, f32[2048,512]{0,1:T(8,128)} %copy.38, bf16[2048,512]{0,1:T(8,128)(2,1)} %copy.37, f32[512]{0:T(512)S(1)} %copy-done.14), kind=kLoop, calls=%fused_computation.23 | loop fusion | flops 10483200 | bytes 10522624 | tf_op jit(solution)/shard_map/transpose(jvp())/reduce_sum | solution.py:28
  135.9 1.7 fusion.76
  138.3 3.3 fusion.82
  141.5 2.3 fusion.22
  143.9 5.1 %fusion.13 = f32[1536,512]{1,0:T(8,128)} fusion(bf16[2048,1536]{1,0:T(8,128)(2,1)S(1)} %bitcast.35, bf16[2048,512]{1,0:T(8,128)(2,1)S(1)} %get-tuple-element.71), kind=kOutput, calls=%fused_computation.41 | convolution fusion | flops 3222011904 | bytes 11534336 | tf_op jit(solution)/shard_map/transpose(jvp())/dot_general | solution.py:34
  149.1 7.0 %fusion.85 = bf16[2048,1536]{1,0:T(8,128)(2,1)} fusion(bf16[2048,512]{1,0:T(8,128)(2,1)} %copy-done.33, bf16[1536,512]{1,0:T(8,128)(2,1)S(1)} %copy-done), kind=kOutput, calls=%fused_computation.159 | convolution fusion | flops 3221225472 | bytes 9961472 | tf_op jit(solution)/shard_map/transpose(jvp())/dot_general | solution.py:34
  156.1 13.8 %scatter_custom_fusion.1 = f32[448,512]{1,0:T(8,128)S(1)} fusion(s32[2048]{0:T(1024)} %param.21, bf16[2048,1536]{1,0:T(8,128)(2,1)} %fusion.85, f32[]{:T(128)} %constant.10.clone.1), kind=kCustom, calls=%fused_computation.26 | custom fusion | flops 2097152 | bytes 3015168 | tf_op jit(solution)/shard_map/scatter-add | solution.py:117
  170.7 2.3 collective-permute-start.4
  173.0 1.3 collective-permute-start.5
  174.3 2.1 collective-permute-start.6
  176.4 2.8 collective-permute-start.7
  179.9 5.0 %all-to-all-start.1 = ((bf16[32,2,512]{2,1,0:T(2,128)(2,1)}), bf16[32,2,512]{2,1,0:T(2,128)(2,1)S(1)}, u32[]{:S(2)}, u32[]{:S(2)}) async-start(bf16[32,2,512]{2,1,0:T(2,128)(2,1)} %convert_element_type.128), calls=%async_computation.1 | async-start | bytes 131072 | tf_op jit(solution)/shard_map/all_to_all | solution.py:140
  185.0 3.9 %slice_add_fusion = bf16[2048,512]{1,0:T(8,128)(2,1)} fusion(bf16[2048,512]{1,0:T(8,128)(2,1)} %param.33, bf16[2048,1536]{1,0:T(8,128)(2,1)} %fusion.85), kind=kLoop, calls=%fused_computation.42 | loop fusion | flops 1048576 | bytes 6291456 | tf_op jit(solution)/shard_map/transpose(jvp())/add_any | solution.py:33
  189.9 15.2 %scatter_custom_fusion.2 = f32[256,512]{1,0:T(8,128)S(1)} fusion(f32[256,512]{1,0:T(8,128)S(1)} %slice_add_fusion.1, s32[2048]{0:T(1024)S(1)} %copy-done.15, bf16[2048,1536]{1,0:T(8,128)(2,1)} %fusion.85), kind=kCustom, calls=%fused_computation.24 | custom fusion | flops 2097152 | bytes 2621440 | tf_op jit(solution)/shard_map/scatter-add | solution.py:114
  205.2 3.9 %copy.39 = bf16[2048,512]{1,0:T(8,128)(2,1)} copy(bf16[2048,512]{0,1:T(8,128)(2,1)} %get-tuple-element.52) | data formatting | bytes 4194304
  209.1 40.3 %all-reduce = (f32[512]{0:T(512)}, f32[512]{0:T(512)}, f32[512]{0:T(512)}, f32[512]{0:T(512)}) all-reduce(f32[512]{0:T(512)S(1)} %copy-done.20, f32[512]{0:T(512)S(1)} %get-tuple-element.36, f32[512]{0:T(512)S(1)} %copy-done.19, f32[512]{0:T(512)S(1)} %get-tuple-element.38), channel_id=1, replica_groups=mesh['lat'=4,'lon'=8] {'lat','lon'}, use_global_device_ids=true, to_apply=%region_18.19 | all-reduce | flops 2048 | bytes 16384 | tf_op jit(solution)/shard_map/psum | solution.py:146
  256.2 64.0 %all-reduce.4.cloned.1.call-done = (f32[1536,512]{1,0:T(8,128)}, f32[512,512]{1,0:T(8,128)}, f32[1024,512]{1,0:T(8,128)}, f32[512,512]{1,0:T(8,128)}) async-done(((f32[1536,512]{1,0:T(8,128)}, f32[512,512]{1,0:T(8,128)}, f32[1024,512]{1,0:T(8,128)}, f32[512,512]{1,0:T(8,128)}), (f32[1536,512]{1,0:T(8,128)}, f32[512,512]{1,0:T(8,128)}, f32[1024,512]{1,0:T(8,128)}, ...) | async-done | bytes 7340048 | tf_op jit(solution)/shard_map/psum | solution.py:146
  320.2 4.0 %copy.58 = f32[1536,512]{1,0:T(8,128)} copy(f32[1536,512]{1,0:T(8,128)} %get-tuple-element.82) | data formatting | bytes 6291456
  325.2 1.3 copy.60
  (134 shorter events, 21.4 us)
Async XLA Ops:
  7.2 62.5 %copy-start = (bf16[1536,512]{1,0:T(8,128)(2,1)S(1)}, bf16[1536,512]{1,0:T(8,128)(2,1)}, u32[]{:S(2)}) copy-start(bf16[1536,512]{1,0:T(8,128)(2,1)} %param.24) | copy-start | bytes 4718596
  7.2 30.6 %copy-start.15 = (s32[2048]{0:T(1024)S(1)}, s32[2048]{0:T(1024)}, u32[]{:S(2)}) copy-start(s32[2048]{0:T(1024)} %param.20) | copy-start | bytes 24580
  8.1 7.0 %copy-start.21 = (s32[32]{0:T(128)}, s32[32]{0:T(128)S(1)}, u32[]{:S(2)}) copy-start(s32[32]{0:T(128)S(1)} %get-tuple-element.65) | copy-start | bytes 388
  8.1 7.0 %copy-start.23 = (s32[32]{0:T(128)}, s32[32]{0:T(128)S(1)}, u32[]{:S(2)}) copy-start(s32[32]{0:T(128)S(1)} %get-tuple-element.64) | copy-start | bytes 388
  8.1 7.0 %copy-start.24 = (s32[32]{0:T(128)}, s32[32]{0:T(128)S(1)}, u32[]{:S(2)}) copy-start(s32[32]{0:T(128)S(1)} %get-tuple-element.63) | copy-start | bytes 388
  8.1 11.0 %copy-start.22 = (s32[32]{0:T(128)}, s32[32]{0:T(128)S(1)}, u32[]{:S(2)}) copy-start(s32[32]{0:T(128)S(1)} %get-tuple-element.62) | copy-start | bytes 388
  9.7 45.8 %collective-permute-start = (bf16[32,512]{1,0:T(8,128)(2,1)S(1)}, bf16[32,512]{1,0:T(8,128)(2,1)S(1)}, u32[]{:S(2)}, u32[]{:S(2)}) collective-permute-start(bf16[32,512]{1,0:T(8,128)(2,1)S(1)} %gather_fusion), channel_id=1, source_target_pairs={{0,8},{8,16},{16,24},{1,9},{9,17},{17,25},{2,10},{10,18},{18,26},{... | collective-permute-start | bytes 98312 | tf_op jit(solution)/shard_map/ppermute | solution.py:18
  13.7 41.8 %collective-permute-start.1 = (bf16[32,512]{1,0:T(8,128)(2,1)S(1)}, bf16[32,512]{1,0:T(8,128)(2,1)S(1)}, u32[]{:S(2)}, u32[]{:S(2)}) collective-permute-start(bf16[32,512]{1,0:T(8,128)(2,1)S(1)} %gather_fusion.1), channel_id=1, source_target_pairs={{8,0},{16,8},{24,16},{9,1},{17,9},{25,17},{10,2},{18,10},{26,18},{... | collective-permute-start | bytes 98312 | tf_op jit(solution)/shard_map/ppermute | solution.py:19
  16.7 38.9 %collective-permute-start.2 = (bf16[32,512]{1,0:T(8,128)(2,1)S(1)}, bf16[32,512]{1,0:T(8,128)(2,1)S(1)}, u32[]{:S(2)}, u32[]{:S(2)}) collective-permute-start(bf16[32,512]{1,0:T(8,128)(2,1)S(1)} %gather_fusion.2), channel_id=1, source_target_pairs={{0,1},{1,2},{2,3},{3,4},{4,5},{5,6},{6,7},{7,0},{8,9},{9,10},{10,1... | collective-permute-start | bytes 98312 | tf_op jit(solution)/shard_map/ppermute | solution.py:18
  20.7 34.9 %collective-permute-start.3 = (bf16[32,512]{1,0:T(8,128)(2,1)S(1)}, bf16[32,512]{1,0:T(8,128)(2,1)S(1)}, u32[]{:S(2)}, u32[]{:S(2)}) collective-permute-start(bf16[32,512]{1,0:T(8,128)(2,1)S(1)} %gather_fusion.3), channel_id=1, source_target_pairs={{1,0},{2,1},{3,2},{4,3},{5,4},{6,5},{7,6},{0,7},{9,8},{10,9},{11,1... | collective-permute-start | bytes 98312 | tf_op jit(solution)/shard_map/ppermute | solution.py:19
  24.7 9.2 %copy-start.17 = (s32[64]{0:T(128)}, s32[64]{0:T(128)S(1)}, u32[]{:S(2)}) copy-start(s32[64]{0:T(128)S(1)} %fusion.71) | copy-start | bytes 772
  27.1 28.5 %all-to-all-start = ((bf16[32,2,512]{2,1,0:T(2,128)(2,1)}), bf16[32,2,512]{2,1,0:T(2,128)(2,1)S(1)}, u32[]{:S(2)}, u32[]{:S(2)}) async-start(bf16[32,2,512]{2,1,0:T(2,128)(2,1)} %reshape.255), calls=%async_computation | async-start | bytes 131072 | tf_op jit(solution)/shard_map/all_to_all | solution.py:82
  32.9 287.2 %all-reduce.4.cloned.1.call-start = ((), (), s32[]{:S(2)}) async-start(), calls=%async_computation.2 | async-start | bytes 14680064 | tf_op jit(solution)/shard_map/psum | solution.py:146
  34.7 7.8 %copy-start.1 = (bf16[256,512]{1,0:T(8,128)(2,1)S(1)}, bf16[256,512]{1,0:T(8,128)(2,1)}, u32[]{:S(2)}) copy-start(bf16[256,512]{1,0:T(8,128)(2,1)} %param.17) | copy-start | bytes 786436
  64.9 3.3 copy-start.6
  69.7 5.5 %copy-start.26 = (bf16[512,512]{1,0:T(8,128)(2,1)S(1)}, bf16[512,512]{1,0:T(8,128)(2,1)}, u32[]{:S(2)}) copy-start(bf16[512,512]{1,0:T(8,128)(2,1)} %param.26) | copy-start | bytes 1572868
  69.7 5.5 %copy-start.29 = (f32[512]{0:T(512)S(1)}, f32[512]{0:T(512)}, u32[]{:S(2)}) copy-start(f32[512]{0:T(512)} %param.25) | copy-start | bytes 6148
  75.3 2.0 copy-start.30
  77.3 7.0 %copy-start.2 = (f32[2048,512]{0,1:T(8,128)}, f32[2048,512]{0,1:T(8,128)S(1)}, u32[]{:S(2)}) copy-start(f32[2048,512]{0,1:T(8,128)S(1)} %get-tuple-element.67) | copy-start | bytes 12582916
  77.3 3.1 copy-start.7
  77.3 3.1 copy-start.14
  84.3 20.7 %copy-start.28 = (f32[512]{0:T(512)S(1)}, f32[512]{0:T(512)}, u32[]{:S(2)}) copy-start(f32[512]{0:T(512)} %param.29) | copy-start | bytes 6148
  89.7 18.7 %copy-start.8 = (bf16[256,512]{1,0:T(8,128)(2,1)S(1)}, bf16[256,512]{1,0:T(8,128)(2,1)}, u32[]{:S(2)}) copy-start(bf16[256,512]{1,0:T(8,128)(2,1)} %param.32) | copy-start | bytes 786436
  89.7 18.7 %copy-start.16 = (f32[512]{0:T(512)S(1)}, f32[512]{0:T(512)}, u32[]{:S(2)}) copy-start(f32[512]{0:T(512)} %param.31) | copy-start | bytes 6148
  105.0 4.7 %copy-start.25 = (bf16[512,512]{1,0:T(8,128)(2,1)S(1)}, bf16[512,512]{1,0:T(8,128)(2,1)}, u32[]{:S(2)}) copy-start(bf16[512,512]{1,0:T(8,128)(2,1)} %param.30) | copy-start | bytes 1572868
  108.7 3.4 %copy-start.11 = (bf16[1024,512]{1,0:T(8,128)(2,1)S(1)}, bf16[1024,512]{1,0:T(8,128)(2,1)}, u32[]{:S(2)}) copy-start(bf16[1024,512]{1,0:T(8,128)(2,1)} %param.28) | copy-start | bytes 3145732
  112.6 10.8 %copy-start.9 = (bf16[256,1024]{1,0:T(8,128)(2,1)}, bf16[256,1024]{1,0:T(8,128)(2,1)S(1)}, u32[]{:S(2)}) copy-start(bf16[256,1024]{1,0:T(8,128)(2,1)S(1)} %fusion.86) | copy-start | bytes 1572868
  128.8 5.8 %copy-start.3 = (f32[2048,512]{0,1:T(8,128)S(1)}, f32[2048,512]{0,1:T(8,128)}, u32[]{:S(2)}) copy-start(f32[2048,512]{0,1:T(8,128)} %copy-done.2) | copy-start | bytes 12582916
  128.8 6.5 %copy-start.4 = (f32[2048,512]{0,1:T(8,128)S(1)}, f32[2048,512]{0,1:T(8,128)}, u32[]{:S(2)}) copy-start(f32[2048,512]{0,1:T(8,128)} %copy.38) | copy-start | bytes 12582916
  128.8 7.1 %copy-start.5 = (bf16[2048,512]{0,1:T(8,128)(2,1)S(1)}, bf16[2048,512]{0,1:T(8,128)(2,1)}, u32[]{:S(2)}) copy-start(bf16[2048,512]{0,1:T(8,128)(2,1)} %copy.37) | copy-start | bytes 6291460
  135.9 1.7 copy-start.27
  135.9 2.4 copy-start.31
  138.3 3.3 copy-start.32
  138.3 5.6 %slice-start = ((s8[6291456]{0:T(1024)(128)(4,1)}), s8[4194304]{0:T(1024)(128)(4,1)S(1)}, s32[]{:S(2)}) async-start(s8[6291456]{0:T(1024)(128)(4,1)} %bitcast.34), calls=%async_computation.3 | async-start | bytes 8388608
  141.5 2.3 copy-start.33
  141.5 2.4 slice-start.1
  170.7 78.8 %collective-permute-start.4 = (bf16[32,512]{1,0:T(8,128)(2,1)}, bf16[32,512]{1,0:T(8,128)(2,1)}, u32[]{:S(2)}, u32[]{:S(2)}) collective-permute-start(bf16[32,512]{1,0:T(8,128)(2,1)} %get-tuple-element.61), channel_id=1, source_target_pairs={{0,8},{8,16},{16,24},{1,9},{9,17},{17,25},{2,10},{10,18},{18,26},{... | collective-permute-start | bytes 98312 | tf_op jit(solution)/shard_map/ppermute | solution.py:18
  173.0 76.4 %collective-permute-start.5 = (bf16[32,512]{1,0:T(8,128)(2,1)}, bf16[32,512]{1,0:T(8,128)(2,1)}, u32[]{:S(2)}, u32[]{:S(2)}) collective-permute-start(bf16[32,512]{1,0:T(8,128)(2,1)} %get-tuple-element.60), channel_id=1, source_target_pairs={{8,0},{16,8},{24,16},{9,1},{17,9},{25,17},{10,2},{18,10},{26,18},{... | collective-permute-start | bytes 98312 | tf_op jit(solution)/shard_map/ppermute | solution.py:19
  174.3 77.6 %collective-permute-start.6 = (bf16[32,512]{1,0:T(8,128)(2,1)}, bf16[32,512]{1,0:T(8,128)(2,1)S(1)}, u32[]{:S(2)}, u32[]{:S(2)}) collective-permute-start(bf16[32,512]{1,0:T(8,128)(2,1)} %get-tuple-element.58), channel_id=1, source_target_pairs={{0,1},{1,2},{2,3},{3,4},{4,5},{5,6},{6,7},{7,0},{8,9},{9,10},{10,1... | collective-permute-start | bytes 98312 | tf_op jit(solution)/shard_map/ppermute | solution.py:18
  176.4 75.5 %collective-permute-start.7 = (bf16[32,512]{1,0:T(8,128)(2,1)}, bf16[32,512]{1,0:T(8,128)(2,1)S(1)}, u32[]{:S(2)}, u32[]{:S(2)}) collective-permute-start(bf16[32,512]{1,0:T(8,128)(2,1)} %get-tuple-element.59), channel_id=1, source_target_pairs={{1,0},{2,1},{3,2},{4,3},{5,4},{6,5},{7,6},{0,7},{9,8},{10,9},{11,1... | collective-permute-start | bytes 98312 | tf_op jit(solution)/shard_map/ppermute | solution.py:19
  179.9 74.3 %all-to-all-start.1 = ((bf16[32,2,512]{2,1,0:T(2,128)(2,1)}), bf16[32,2,512]{2,1,0:T(2,128)(2,1)S(1)}, u32[]{:S(2)}, u32[]{:S(2)}) async-start(bf16[32,2,512]{2,1,0:T(2,128)(2,1)} %convert_element_type.128), calls=%async_computation.1 | async-start | bytes 131072 | tf_op jit(solution)/shard_map/all_to_all | solution.py:140
  189.9 19.2 %copy-start.19 = (f32[512]{0:T(512)S(1)}, f32[512]{0:T(512)}, u32[]{:S(2)}) copy-start(f32[512]{0:T(512)} %get-tuple-element.72) | copy-start | bytes 6148
  189.9 19.2 %copy-start.20 = (f32[512]{0:T(512)S(1)}, f32[512]{0:T(512)}, u32[]{:S(2)}) copy-start(f32[512]{0:T(512)} %get-tuple-element.70) | copy-start | bytes 6148
  189.9 64.3 %copy-start.18 = (s32[64]{0:T(128)S(1)}, s32[64]{0:T(128)}, u32[]{:S(2)}) copy-start(s32[64]{0:T(128)} %copy-done.17) | copy-start | bytes 772
  320.2 4.0 %copy-start.13 = (f32[512,512]{1,0:T(8,128)S(1)}, f32[512,512]{1,0:T(8,128)}, u32[]{:S(2)}) copy-start(f32[512,512]{1,0:T(8,128)} %get-tuple-element.84) | copy-start | bytes 3145732
  320.2 5.0 %copy-start.10 = (f32[1024,512]{1,0:T(8,128)S(1)}, f32[1024,512]{1,0:T(8,128)}, u32[]{:S(2)}) copy-start(f32[1024,512]{1,0:T(8,128)} %get-tuple-element.86) | copy-start | bytes 6291460
  324.2 2.3 copy-start.12
Sparse Core Ops, SparseCore 0:
  149.2 170.8 all-reduce.3
where the time goes:
time: 336 us; the launch traced here: 334 us
  local copies, waits for them, and re-layouts  82.2 us (24%)
  other arithmetic  71.1 us (21%)
  waiting for transfers between devices  64 us (19%)
  blocking collectives  40.3 us (12%)
  matrix products  32.6 us (10%)
  starting transfers between devices  28.6 us (9%)
  between operations  15.3 us (5%)
    psum x1, waiting for transfers between devices, shards(): summed = lax.psum(every_grad, ('lat', 'lon'))  64 us
    psum x1, blocking collectives, shards(): summed = lax.psum(every_grad, ('lat', 'lon'))  40.3 us
    unnamed x87, local copies, waits for them, and re-layouts  32.3 us
    dot_general x3, matrix products, edge_update(): jnp.dot(joined, weight_in, preferred_element_type=jnp.float32) + bias_in  17.6 us
    scatter-add x1, other arithmetic, shards(): jax.ops.segment_sum(message, receiver, node_rows, indices_are_sorted=True)  15.2 us
    scatter-add x1, other arithmetic, shards(): jax.ops.segment_sum(from_receive.astype(jnp.float32), receiver, node_rows...  15.2 us
    gather x2, local copies, waits for them, and re-layouts, shards(): from_gathered.astype(jnp.float32)[receiver]  14.3 us
    scatter-add x1, other arithmetic, shards(): jax.ops.segment_sum(from_send.astype(jnp.float32), sender, node_rows + 4...  13.8 us
  transfers between devices with their start and end apart: 11, of which 1 were waited for; matrix products, arithmetic and copies ran while one was open for 25% of the time, Pallas kernels for 0%

commit v1 on v0

v1 whole, which is shorter than its diff:
```python
import math
from functools import partial

import jax
import jax.numpy as jnp
from jax import lax
from jax.experimental import pallas as pl
from jax.experimental.pallas import tpu as pltpu
from jax.sharding import PartitionSpec as P

EPSILON = 1e-05
LANES = 128
TILE = 1024
STRIP = 512
SMALL = 16
CHUNK = 64
F32 = jnp.float32
BF16 = jnp.bfloat16


def dot(a, b):
    return lax.dot_general(a, b, (((1,), (0,)), ((), ())), preferred_element_type=F32)


def dot_right_t(a, b):
    return lax.dot_general(a, b, (((1,), (1,)), ((), ())), preferred_element_type=F32)


def dot_left_t(a, b):
    return lax.dot_general(a, b, (((0,), (0,)), ((), ())), preferred_element_type=F32)


def strips(rows):
    return [slice(start, start + STRIP) for start in range(0, rows, STRIP)]


def chunks(strip):
    return [slice(start, start + CHUNK) for start in range(strip.start, strip.stop, CHUNK)]


def spread_index(index_row):
    return jnp.transpose(jnp.broadcast_to(index_row, (LANES, index_row.shape[1])))


def lane_hot(column, width):
    lane = lax.broadcasted_iota(jnp.int32, column.shape, 1)
    parts = [
        jnp.where(column == lane + start, 1.0, 0.0).astype(BF16)
        for start in range(0, width, LANES)
    ]
    return jnp.concatenate(parts, axis=1)


def sublane_hot(index_row, width):
    row = lax.broadcasted_iota(jnp.int32, (width, index_row.shape[1]), 0)
    return jnp.where(row == index_row, 1.0, 0.0).astype(BF16)


def sigmoid(values):
    return 0.5 * jnp.tanh(0.5 * values) + 0.5


def normed(values):
    row_mean = jnp.mean(values, axis=-1, keepdims=True)
    centered = values - row_mean
    variance = jnp.mean(centered * centered, axis=-1, keepdims=True)
    inverse = lax.rsqrt(variance + EPSILON)
    return centered * inverse, inverse


def norm_back(cot, gain, hat, inverse):
    product = cot * hat
    scaled = cot * gain
    mean_scaled = jnp.mean(scaled, axis=-1, keepdims=True)
    mean_product = jnp.mean(product * gain, axis=-1, keepdims=True)
    return inverse * (scaled - mean_scaled - hat * mean_product), product


def small_rows(bias_terms, gain_terms, first):
    row = lax.broadcasted_iota(jnp.int32, (SMALL, bias_terms.shape[1]), 0) // 4
    bias, gain = (jnp.sum(terms, axis=0, keepdims=True) for terms in (bias_terms, gain_terms))
    return jnp.where(row == first, bias, jnp.where(row == first + 1, gain, 0.0))


def half_of(number, half):
    return pl.ds(pl.multiple_of(number * half, 16), half)


def halve(total_ref, axis, keep_ref, send_ref):
    place = lax.axis_index(axis)
    half = keep_ref.shape[0] - SMALL
    for target, number in ((keep_ref, place), (send_ref, 1 - place)):
        target[:half, :] = total_ref[half_of(number, half), :]
        target[half:, :] = total_ref[2 * half :, :]


def add(one, other):
    return (one.astype(F32) + other.astype(F32)).astype(BF16)


def block_number(axes, flips):
    number = 0
    for axis in axes:
        own = lax.axis_index(axis)
        number = 2 * number + (1 - own if axis in flips else own)
    return number


def plane_kernel(axes, sides, node_half, keep, got, *targets):
    node_keep, edge_keep = keep.at[:node_half, :], keep.at[node_half:, :]
    node_got, edge_got = got.at[:node_half, :], got.at[node_half:, :]
    edge_rows, node_rows = edge_keep.shape[0] - SMALL, node_keep.shape[0] - SMALL
    edge_part, node_part = edge_rows // len(sides), node_rows // len(sides)
    both = edge_part + node_part
    small = add(
        edge_keep[edge_rows:, :].astype(F32) + edge_got[edge_rows:, :].astype(F32),
        node_keep[node_rows:, :].astype(F32) + node_got[node_rows:, :].astype(F32),
    )
    for flips, target in zip(sides, targets):
        number = block_number(axes, flips)
        rows = half_of(number, edge_part)
        target[:edge_part, :] = add(edge_keep[rows, :], edge_got[rows, :])
        rows = half_of(number, node_part)
        target[edge_part:both, :] = add(node_keep[rows, :], node_got[rows, :])
        end = target.shape[0] - SMALL
        if end > both:
            target[both:end, :] = jnp.zeros((end - both, target.shape[1]), BF16)
        target[end:, :] = small


def line_kernel(sources, *refs):
    parts, targets, total_ref = refs[:sources], refs[sources:-1], refs[-1]
    total = parts[0][...].astype(F32)
    for part in parts[1:]:
        total += part[...].astype(F32)
    total_ref[...] = total.astype(BF16)
    count = len(targets)
    part = targets[0].shape[0] - SMALL
    place = lax.axis_index("z")
    for ahead, target in enumerate(targets):
        target[:part, :] = total_ref[half_of((place + ahead) % count, part), :]
        target[part:, :] = total_ref[count * part :, :]


def total_kernel(*refs):
    parts, (own_ref, small_ref) = refs[:-2], refs[-2:]
    total = parts[0][...].astype(F32)
    for part in parts[1:]:
        total += part[...].astype(F32)
    rows = own_ref.shape[0]
    own_ref[...] = total[:rows, :].astype(BF16)
    small_ref[...] = total[rows:, :]


def join_kernel(*refs):
    parts, (own_ref, top_ref, bottom_ref) = refs[:-3], refs[-3:]
    place = lax.axis_index("z")
    for step, part in enumerate(parts):
        number = lax.bitwise_xor(place, jnp.int32(step))
        own_ref[half_of(number, part.shape[0]), :] = part[...]
    half = top_ref.shape[0]
    top_ref[...] = own_ref[:half, :]
    bottom_ref[...] = own_ref[half:, :]


def finish_kernel(axes, edge_part, node_part, held, *refs):
    pieces, refs = refs[: len(held)], refs[len(held) :]
    wide_ref, sems = refs[-2:]
    if len(refs) == 11:
        small, vectors, refs = refs[0], refs[5:9], refs[1:5] + refs[9:]
        for number, target in enumerate(vectors):
            target[...] = small[4 * number : 4 * number + 4, :][0]
    edge_in, edge_out, node_in, node_out = refs[-6:-2]
    moves, start = [], 0
    for (flips, first), piece in zip(held, pieces):
        last = first + piece.shape[0]
        number = block_number(("core",) + axes, flips)
        for low, size, (one, two) in (
            (0, edge_part, (edge_in, edge_out)),
            (edge_part, node_part, (node_in, node_out)),
        ):
            unit = math.gcd(size, one.shape[0])
            for base in range(low, low + size, unit):
                begin, end = max(first, base), min(last, base + unit)
                if begin >= end:
                    continue
                rows = end - begin
                wide_ref[start : start + rows, :] = piece[begin - first : end - first, :].astype(F32)
                place, split = number * size + base - low, one.shape[0]
                source = wide_ref.at[pl.ds(start, rows), :]
                sem = sems.at[len(moves)]

                def copy(target, row, source=source, sem=sem, rows=rows):
                    into = target.at[pl.ds(pl.multiple_of(row, 8), rows), :]
                    return pltpu.make_async_copy(source, into, sem)

                move = (copy, place < split, one, two, place + begin - base, split)
                moves.append(move)
                run(move, "start")
                start += rows
    for move in moves:
        run(move, "wait")


def run(move, action):
    copy, inside, one, two, row, split = move

    @pl.when(inside)
    def _():
        getattr(copy(one, row), action)()

    @pl.when(jnp.logical_not(inside))
    def _():
        getattr(copy(two, row - split), action)()


def spread_rows(target, slot, rows):
    parts = rows.shape[1] // LANES
    stride = target.shape[0] // rows.shape[0]
    for part in range(parts):
        target[pl.ds(slot * parts + part, rows.shape[0], stride=stride), :] = rows[
            :, part * LANES : (part + 1) * LANES
        ]


def block_rows(source, slot, peers, width):
    parts = width // LANES
    stride = source.shape[0] // peers
    return jnp.concatenate(
        [source[pl.ds(slot * parts + part, peers, stride=stride), :] for part in range(parts)],
        axis=1,
    )


def towards(axes, step):
    return 1 - (lax.axis_index(axes) + step) % 2


def pick_kernel(bands, tiles, halo_ref, far_ref, nodes_ref, far_out_ref, *rims):
    count = nodes_ref.shape[0]
    nodes = nodes_ref[...]
    for number, rim in enumerate(rims):
        axes, first = ((bands, 0), (tiles, 2))[number // 2]
        chosen = halo_ref[0, first : first + 1, :]
        after = halo_ref[0, first + 1 : first + 2, :]
        chosen = jnp.where(towards(axes, number % 2) == 1, after, chosen)
        rim[...] = dot_left_t(sublane_hot(chosen, count), nodes).astype(BF16)
    for slot in range(far_ref.shape[1]):
        hot = sublane_hot(far_ref[0, slot : slot + 1, :], count)
        spread_rows(far_out_ref, slot, dot_left_t(hot, nodes))


def far_place(sender, near, peers, capacity):
    far = sender - near
    return jnp.where(far < 0, sender, near + far % capacity * peers + far // capacity)


def forward_pass(
    step,
    last,
    peers,
    capacity,
    bands,
    tiles,
    count_ref,
    sender_ref,
    receiver_ref,
    edges_ref,
    nodes_ref,
    band_even_ref,
    band_odd_ref,
    tile_even_ref,
    tile_odd_ref,
    far_ref,
    weight_in_ref,
    bias_ref,
    weight_out_ref,
    gain_ref,
    node_weight_in_ref,
    node_bias_ref,
    node_weight_out_ref,
    node_gain_ref,
    cot_nodes_ref,
    edge_out_ref,
    active_ref,
    slope_ref,
    hat_ref,
    inverse_ref,
    table_ref,
    node_out_ref,
    from_gathered_ref,
    from_node_ref,
    keep_ref,
    send_ref,
    projected_ref,
    gathered_ref,
    grads_ref,
    hot_ref,
    wide_ref,
    message_ref,
):
    tile, width = edges_ref.shape
    node_rows = nodes_ref.shape[0]
    slots = table_ref.shape[0]

    @pl.when(step == 0)
    def _():
        table_ref[...] = jnp.zeros_like(table_ref)
        place = 0
        table_ref[:node_rows, :] = nodes_ref[...]
        place += node_rows
        rims = (band_even_ref, band_odd_ref, tile_even_ref, tile_odd_ref)
        for number, rim in enumerate(rims):
            axes = (bands, tiles)[number // 2]
            border = rim.shape[0]
            slot = number // 2 * 2 + towards(axes, number % 2)
            rows = pl.ds(pl.multiple_of(place + slot * border, 32), border)
            table_ref[rows, :] = rim[...]
        place += 4 * border
        for slot in range(capacity):
            table_ref[place : place + peers, :] = block_rows(far_ref, slot, peers, width).astype(
                BF16
            )
            place += peers
        projected_ref[:slots, :] = dot(
            table_ref[...], weight_in_ref[width : 2 * width, :]
        ).astype(BF16)
        projected_ref[slots:, :] = dot(
            nodes_ref[...], weight_in_ref[2 * width :, :]
        ).astype(BF16)
        gathered_ref[...] = jnp.zeros_like(gathered_ref)

    near = node_rows + 4 * band_even_ref.shape[0]
    sender = far_place(sender_ref[...], near, peers, capacity)
    receiver = receiver_ref[...]
    halves = strips(tile)

    def gather(strip):
        senders = spread_index(sender[:, strip])
        receivers = spread_index(receiver[:, strip])
        for rows in chunks(strip):
            here = slice(rows.start - strip.start, rows.stop - strip.start)
            hot_ref[rows, :slots] = lane_hot(senders[here, :], slots)
            hot_ref[rows, slots:] = lane_hot(receivers[here, :], node_rows)
        wide_ref[strip, :] = dot(edges_ref[strip, :], weight_in_ref[:width, :]) + dot(
            hot_ref[strip, :], projected_ref[...]
        )

    def activate(strip):
        for rows in chunks(strip):
            first = wide_ref[rows, :] + bias_ref[...]
            gate = sigmoid(first)
            active = first * gate
            message_ref[rows, :] = active.astype(BF16)
            active_ref[rows, :] = active.astype(BF16)
            slope_ref[rows, :] = (gate + active * (1.0 - gate)).astype(BF16)
        wide_ref[strip, :] = dot(message_ref[strip, :], weight_out_ref[...])

    def send(strip):
        for rows in chunks(strip):
            hat, inverse = normed(wide_ref[rows, :])
            hat_ref[rows, :] = hat.astype(BF16)
            inverse_ref[rows, :] = jnp.broadcast_to(inverse, (CHUNK, inverse_ref.shape[1]))
            place = lax.broadcasted_iota(jnp.int32, (CHUNK, 1), 0) + (step * tile + rows.start)
            message = jnp.where(place < count_ref[0], hat * gain_ref[...], 0.0)
            message_ref[rows, :] = message.astype(BF16)
            edge_out_ref[rows, :] = (edges_ref[rows, :].astype(F32) + message).astype(BF16)

    for work in (gather, activate, send):
        for strip in halves:
            work(strip)
    gathered_ref[...] += dot(sublane_hot(receiver, node_rows), message_ref[...])

    @pl.when(step == last)
    def _():
        nodes = nodes_ref[...]
        gathered = gathered_ref[...].astype(BF16)
        first = (
            dot(nodes, node_weight_in_ref[:width, :])
            + dot(gathered, node_weight_in_ref[width:, :])
            + node_bias_ref[...]
        )
        gate = sigmoid(first)
        active_wide = first * gate
        slope = gate + active_wide * (1.0 - gate)
        active = active_wide.astype(BF16)
        hat, inverse = normed(dot(active, node_weight_out_ref[...]))
        gain = node_gain_ref[...]
        node_out_ref[...] = (nodes.astype(F32) + hat * gain).astype(BF16)
        cot = cot_nodes_ref[...].astype(F32)
        back, product = norm_back(cot, gain, hat, inverse)
        second_back = back.astype(BF16)
        first_wide = dot_right_t(second_back, node_weight_out_ref[...]) * slope
        first_back = first_wide.astype(BF16)
        from_node_ref[...] = cot + dot_right_t(first_back, node_weight_in_ref[:width, :])
        from_gathered_ref[...] = dot_right_t(
            first_back, node_weight_in_ref[width:, :]
        ).astype(BF16)
        grads_ref[:width, :] = dot_left_t(nodes, first_back).astype(BF16)
        grads_ref[width : 2 * width, :] = dot_left_t(gathered, first_back).astype(BF16)
        grads_ref[2 * width : 3 * width, :] = dot_left_t(active, second_back).astype(BF16)
        grads_ref[3 * width :, :] = small_rows(first_wide, product, 2).astype(BF16)
        halve(grads_ref, "core", keep_ref, send_ref)


def backward_pass(
    step,
    last,
    peers,
    capacity,
    near,
    bands,
    tiles,
    count_ref,
    sender_ref,
    receiver_ref,
    edges_ref,
    cot_ref,
    active_ref,
    slope_ref,
    hat_ref,
    inverse_ref,
    table_ref,
    from_gathered_ref,
    from_node_ref,
    weight_in_ref,
    weight_out_ref,
    gain_ref,
    edge_grad_ref,
    totals_ref,
    back_far_ref,
    band_even_ref,
    band_odd_ref,
    tile_even_ref,
    tile_odd_ref,
    keep_ref,
    send_ref,
    sums_ref,
    in_sum_ref,
    out_sum_ref,
    gain_sum_ref,
    grads_ref,
    wide_ref,
    second_ref,
    first_ref,
):
    tile, width = edges_ref.shape
    node_rows = from_gathered_ref.shape[0]
    slots = table_ref.shape[0]

    @pl.when(step == 0)
    def _():
        sums_ref[...] = jnp.zeros_like(sums_ref)
        in_sum_ref[...] = jnp.zeros_like(in_sum_ref)
        out_sum_ref[...] = jnp.zeros_like(out_sum_ref)
        gain_sum_ref[...] = jnp.zeros_like(gain_sum_ref)

    sender = far_place(sender_ref[...], near, peers, capacity)
    receiver = receiver_ref[...]
    halves = strips(tile)
    for strip in halves:
        hot = lane_hot(spread_index(receiver[:, strip]), node_rows)
        wide_ref[strip, :] = dot(hot, from_gathered_ref[...])

    def normalize(strip):
        gain_sum = gain_sum_ref[...]
        for rows in chunks(strip):
            place = lax.broadcasted_iota(jnp.int32, (CHUNK, 1), 0) + (step * tile + rows.start)
            cot = cot_ref[rows, :].astype(F32) + wide_ref[rows, :]
            cot = jnp.where(place < count_ref[0], cot, 0.0)
            hat = hat_ref[rows, :].astype(F32)
            back, product = norm_back(cot, gain_ref[...], hat, inverse_ref[rows, 0:1])
            gain_sum += jnp.sum(product.reshape(CHUNK // 8, 8, width), axis=0)
            second_ref[rows, :] = back.astype(BF16)
        gain_sum_ref[...] = gain_sum
        wide_ref[strip, :] = dot_right_t(second_ref[strip, :], weight_out_ref[...])

    def activate(strip):
        for rows in chunks(strip):
            first_ref[rows, :] = (wide_ref[rows, :] * slope_ref[rows, :].astype(F32)).astype(BF16)
        wide_ref[strip, :] = dot_right_t(first_ref[strip, :], weight_in_ref[:width, :])

    for work in (normalize, activate):
        for strip in halves:
            work(strip)
    out_sum_ref[...] += dot_left_t(active_ref[...], second_ref[...])
    for rows in chunks(slice(0, tile)):
        edge_grad_ref[rows, :] = (cot_ref[rows, :].astype(F32) + wide_ref[rows, :]).astype(BF16)
    first_back = first_ref[...]
    in_sum_ref[...] += dot_left_t(edges_ref[...], first_back)
    sums_ref[:slots, :] += dot(sublane_hot(sender, slots), first_back)
    sums_ref[slots:, :] += dot(sublane_hot(receiver, node_rows), first_back)

    @pl.when(step == last)
    def _():
        sent = sums_ref[:slots, :].astype(BF16)
        received_wide = sums_ref[slots:, :]
        received = received_wide.astype(BF16)
        grads_ref[:width, :] = in_sum_ref[...].astype(BF16)
        grads_ref[width : 2 * width, :] = dot_left_t(table_ref[...], sent).astype(BF16)
        grads_ref[2 * width : 3 * width, :] = dot_left_t(
            table_ref[:node_rows, :], received
        ).astype(BF16)
        grads_ref[3 * width : 4 * width, :] = out_sum_ref[...].astype(BF16)
        grads_ref[4 * width :, :] = small_rows(received_wide, gain_sum_ref[...], 0).astype(BF16)
        halve(grads_ref, "core", keep_ref, send_ref)
        sent_back = dot_right_t(sent, weight_in_ref[width : 2 * width, :])
        totals_ref[...] = (
            from_node_ref[...]
            + dot_right_t(received, weight_in_ref[2 * width :, :])
            + sent_back[:node_rows, :]
        )
        place = node_rows
        rims = (band_even_ref, band_odd_ref, tile_even_ref, tile_odd_ref)
        for number, rim in enumerate(rims):
            axes, first = ((bands, place), (tiles, place + 2 * rim.shape[0]))[number // 2]
            before = sent_back[first : first + rim.shape[0], :]
            after = sent_back[first + rim.shape[0] : first + 2 * rim.shape[0], :]
            rim[...] = jnp.where(towards(axes, number % 2) == 1, after, before).astype(BF16)
        place += 4 * rims[0].shape[0]
        for slot in range(capacity):
            spread_rows(back_far_ref, slot, sent_back[place : place + peers, :])
            place += peers


def passes_kernel(peers, capacity, near, bands, tiles, *refs):
    ins, outs, scratch = refs[:20], refs[20:31], refs[31:]
    count, sender, receiver, edges, cot = ins[:5]
    nodes, *halo, weight_in, bias, weight_out, gain = ins[5:15]
    edge_out, edge_grad, node_out, totals, back_far, *back_rims, keep, send = outs
    active, slope, hat, inverse, table, from_gathered, from_node = scratch[:7]
    projected, gathered, grads, hot, wide, second, first, sums, in_sum, out_sum, gain_sum = scratch[7:]
    tile, width = edges.shape
    steps = pl.num_programs(0) // 2
    step = lax.rem(pl.program_id(0), steps)
    rows = pl.ds(pl.multiple_of(step * tile, tile), tile)
    saved = [ref.at[rows, :] for ref in (active, slope, hat, inverse)]
    node_half = 3 * width // 2 + SMALL
    node_ends = [ref.at[:node_half, :] for ref in (keep, send)]
    edge_ends = [ref.at[node_half:, :] for ref in (keep, send)]

    @pl.when(pl.program_id(0) < steps)
    def _():
        forward_pass(
            step,
            steps - 1,
            peers,
            capacity,
            bands,
            tiles,
            count,
            sender,
            receiver,
            edges,
            nodes,
            *halo,
            weight_in,
            bias,
            weight_out,
            gain,
            *ins[15:],
            edge_out,
            *saved,
            table,
            node_out,
            from_gathered,
            from_node,
            *node_ends,
            projected,
            gathered,
            grads.at[: 3 * width + SMALL, :],
            hot,
            wide,
            second,
        )

    @pl.when(pl.program_id(0) >= steps)
    def _():
        backward_pass(
            step,
            steps - 1,
            peers,
            capacity,
            near,
            bands,
            tiles,
            count,
            sender,
            receiver,
            edges,
            cot,
            *saved,
            table,
            from_gathered,
            from_node,
            weight_in,
            weight_out,
            gain,
            edge_grad,
            totals,
            back_far,
            *back_rims,
            *edge_ends,
            sums,
            in_sum,
            out_sum,
            gain_sum,
            grads,
            wide,
            second,
            first,
        )


def return_kernel(bands, tiles, halo_ref, far_ref, totals_ref, returned_ref, *refs):
    rims, out_ref = refs[:-1], refs[-1]
    count, width = totals_ref.shape
    capacity, peers = far_ref.shape[1:]
    total = totals_ref[...]
    for number, rim in enumerate(rims):
        axes, first = ((bands, 0), (tiles, 2))[number // 2]
        chosen = halo_ref[0, first : first + 1, :]
        after = halo_ref[0, first + 1 : first + 2, :]
        chosen = jnp.where(towards(axes, number % 2) == 1, after, chosen)
        total += dot(sublane_hot(chosen, count), rim[...])
    for slot in range(capacity):
        hot = sublane_hot(far_ref[0, slot : slot + 1, :], count)
        total += dot(hot, block_rows(returned_ref, slot, peers, width).astype(BF16))
    out_ref[...] = total.astype(BF16)


def swap(array, axes, step, wrap):
    size = lax.axis_size(axes)
    pairs = []
    for low in range(step, size if wrap else size - 1, 2):
        high = (low + 1) % size
        pairs += [(low, high), (high, low)]
    return lax.ppermute(array, axes, pairs)


def after(arrays, *others):
    return lax.optimization_barrier((arrays, others))[0]


def limits(megabytes=62):
    return pltpu.CompilerParams(
        dimension_semantics=("arbitrary",), vmem_limit_bytes=megabytes * 2**20
    )


def shards(
    x_axes,
    y_axes,
    node_latents,
    edge_latents,
    edge_count,
    receiver,
    sender,
    halo_send,
    far_send,
    edge_weight_in,
    edge_bias,
    edge_weight_out,
    edge_gain,
    node_weight_in,
    node_bias,
    node_weight_out,
    node_gain,
    cot_nodes,
    cot_edges,
):
    node_rows, width = node_latents.shape
    edge_rows = edge_latents.shape[0]
    border = halo_send.shape[2]
    peers = far_send.shape[1]
    capacity = far_send.shape[2]
    rims = 4 * border
    fars = peers * capacity
    used = node_rows + rims + fars
    slots = -(-used // LANES) * LANES
    tile = TILE
    steps = edge_rows // tile

    far_send = jnp.swapaxes(far_send, 1, 2)
    sender = sender.reshape(1, edge_rows)
    receiver = receiver.reshape(1, edge_rows)
    bands = (*x_axes, "core")
    tiles = ("z", *y_axes)
    everyone = bands + tiles

    def exchanged(blocks):
        parts = blocks.reshape(peers, -1, LANES)
        return lax.all_to_all(parts, everyone, split_axis=0, concat_axis=0, tiled=True).reshape(
            -1, LANES
        )

    def call(kernel, name, out_shape, *args, scratch=()):
        return pl.pallas_call(
            kernel,
            out_shape=out_shape,
            scratch_shapes=scratch,
            compiler_params=pltpu.CompilerParams(vmem_limit_bytes=62 * 2**20),
            name=name,
        )(*args)

    def packed(*shape):
        return jax.ShapeDtypeStruct(shape, BF16)

    def wide(*shape):
        return jax.ShapeDtypeStruct(shape, F32)

    def across(array, axes):
        last = 2 ** len(axes) - 1
        return lax.ppermute(array, axes, [(i, last - i) for i in range(last + 1)])

    def ahead(array, step):
        size = lax.axis_size("z")
        return lax.ppermute(array, "z", [(i, (i + step) % size) for i in range(size)])

    rim_shape = jax.ShapeDtypeStruct((border, width), BF16)
    far_shape = jax.ShapeDtypeStruct((fars * width // LANES, LANES), F32)
    far_rows, *rim_rows = call(
        partial(pick_kernel, bands, tiles),
        "pick",
        (far_shape,) + (rim_shape,) * 4,
        halo_send,
        far_send,
        node_latents,
    )
    def swapped(rims):
        return [
            swap(rims[0], bands, 0, False),
            swap(rims[1], bands, 1, False),
            swap(rims[2], tiles, 0, True),
            swap(rims[3], tiles, 1, True),
        ]

    got_rims = swapped(rim_rows)
    incoming = exchanged(far_rows)

    def whole(*shape):
        return pl.BlockSpec(shape, lambda i: (0,) * len(shape))

    both = pl.BlockSpec((tile, width), lambda i: (i % steps, 0))
    ahead_only = pl.BlockSpec((tile, width), lambda i: (jnp.minimum(i, steps - 1), 0))
    back_only = pl.BlockSpec((tile, width), lambda i: (jnp.maximum(i - steps, 0), 0))
    index_spec = pl.BlockSpec((1, tile), lambda i: (0, i % steps))
    scalar = pl.BlockSpec(memory_space=pltpu.SMEM)
    rim_spec = whole(border, width)
    far_spec = whole(*far_shape.shape)
    line, node_spec, square = whole(1, width), whole(node_rows, width), whole(width, width)
    node_half = 3 * width // 2 + SMALL
    edge_half = 4 * width // 2 + SMALL
    flat = packed(edge_rows, width)
    core_half = packed(node_half + edge_half, width)
    (edge_out, edge_grad, node_out, totals, back_far, *back_rims, keep, send) = pl.pallas_call(
        partial(passes_kernel, peers, capacity, node_rows + rims, bands, tiles),
        grid=(2 * steps,),
        in_specs=[scalar, index_spec, index_spec, both, back_only, node_spec]
        + [rim_spec] * 4
        + [far_spec, whole(3 * width, width), line, square, line]
        + [whole(2 * width, width), line, square, line, node_spec],
        out_specs=(ahead_only, back_only, node_spec, node_spec, far_spec)
        + (rim_spec,) * 4
        + (whole(*core_half.shape),) * 2,
        out_shape=(flat, flat, packed(node_rows, width), wide(node_rows, width), far_shape)
        + (rim_shape,) * 4
        + (core_half,) * 2,
        scratch_shapes=[
            pltpu.VMEM((edge_rows, width), BF16),
            pltpu.VMEM((edge_rows, width), BF16),
            pltpu.VMEM((edge_rows, width), BF16),
            pltpu.VMEM((edge_rows, LANES), F32),
            pltpu.VMEM((slots, width), BF16),
            pltpu.VMEM((node_rows, width), BF16),
            pltpu.VMEM((node_rows, width), F32),
            pltpu.VMEM((slots + node_rows, width), BF16),
            pltpu.VMEM((node_rows, width), F32),
            pltpu.VMEM((4 * width + SMALL, width), BF16),
            pltpu.VMEM((tile, slots + node_rows), BF16),
            pltpu.VMEM((tile, width), F32),
            pltpu.VMEM((tile, width), BF16),
            pltpu.VMEM((tile, width), BF16),
            pltpu.VMEM((slots + node_rows, width), F32),
            pltpu.VMEM((width, width), F32),
            pltpu.VMEM((width, width), F32),
            pltpu.VMEM((8, width), F32),
        ],
        compiler_params=limits(),
        cost_estimate=pl.CostEstimate(
            flops=2 * 10**10, bytes_accessed=2 * 10**7, transcendentals=10**6
        ),
        name="passes",
    )(
        edge_count,
        sender,
        receiver,
        edge_latents,
        cot_edges,
        node_latents,
        *got_rims,
        incoming,
        edge_weight_in,
        edge_bias.reshape(1, width),
        edge_weight_out,
        edge_gain.reshape(1, width),
        node_weight_in,
        node_bias.reshape(1, width),
        node_weight_out,
        node_gain.reshape(1, width),
        cot_nodes,
    )
    core_got = across(send, ("core",))
    plane = x_axes + y_axes
    sides = [()]
    for axis in plane:
        sides += [flips + (axis,) for flips in sides]
    depth = lax.axis_size("z")
    edge_part = (edge_half - SMALL) // len(sides)
    node_part = (node_half - SMALL) // len(sides)
    part = -(-(edge_part + node_part) // (16 * depth)) * 16
    parts = call(
        partial(plane_kernel, plane, sides, node_half),
        "plane",
        (packed(part * depth + SMALL, width),) * len(sides),
        keep,
        core_got,
    )
    got = [across(array, flips) for array, flips in zip(parts[1:], sides[1:])]

    back_far, back_rims = after((back_far, back_rims), parts)
    returned_rims = swapped(back_rims)
    returned = exchanged(back_far)
    parts = call(
        partial(line_kernel, len(sides)),
        "line",
        (packed(part + SMALL, width),) * depth,
        *after((parts[0], *got), returned, returned_rims),
        scratch=[pltpu.VMEM((part * depth + SMALL, width), BF16)],
    )
    got = [ahead(parts[step], step) for step in range(1, depth)]
    own, small = call(
        total_kernel, "total", (packed(part, width), wide(SMALL, width)), parts[0], *got
    )
    lines, bit = {0: own}, depth // 2
    while bit:
        for step, piece in list(lines.items()):
            lines[step + bit] = lax.ppermute(piece, "z", [(i, i ^ bit) for i in range(depth)])
        bit //= 2
    middle = part * depth // 2
    own, top, bottom = call(
        join_kernel,
        "join",
        (packed(2 * middle, width), packed(middle, width), packed(middle, width)),
        *(lines[step] for step in range(depth)),
    )
    grad_nodes = call(
        partial(return_kernel, bands, tiles),
        "returned",
        packed(node_rows, width),
        *after((halo_send, far_send, totals, returned, *returned_rims), own),
    )

    copies = edge_part // math.gcd(edge_part, 3 * width) + node_part // math.gcd(node_part, 2 * width)
    anywhere, here = pl.BlockSpec(memory_space=pl.ANY), pl.BlockSpec(memory_space=pltpu.VMEM)
    whole_grads = (wide(3 * width, width), wide(width, width))
    whole_grads += (wide(2 * width, width), wide(width, width))

    def finished(pieces, extra):
        rows = sum(piece.shape[0] for piece in pieces.values())
        first = len(extra) == 1
        return pl.pallas_call(
            partial(finish_kernel, plane, edge_part, node_part, tuple(pieces.keys())),
            out_shape=whole_grads + (wide(width),) * (4 if first else 0),
            in_specs=[here] * len(pieces) + ([here] if first else [anywhere] * 4),
            out_specs=(anywhere,) * 4 + (here,) * (4 if first else 0),
            input_output_aliases={} if first else {len(pieces) + i: i for i in range(4)},
            scratch_shapes=[
                pltpu.VMEM((rows, width), F32),
                pltpu.SemaphoreType.DMA((copies * len(pieces),)),
            ],
            compiler_params=pltpu.CompilerParams(vmem_limit_bytes=62 * 2**20),
            name="finish",
        )(*pieces.values(), *extra)

    held = {((), 0): own}
    if len(plane) == 2:
        one, two = plane
        held[(one,), middle] = across(bottom, (one,))
        held[(two,), 0] = across(top, (two,))
        held[(one,), 0] = across(top, (one,))
        held[(two,), middle] = across(bottom, (two,))
        late = {
            (plane, 0): across(held[(two,), 0], (one,)),
            (plane, middle): across(held[(one,), middle], (two,)),
        }
        for flips in ((one,), (two,)):
            for first in (0, middle):
                late[flips + ("core",), first] = across(held[flips, first], ("core",))
        held[("core",), 0] = across(own, ("core",))
        *grads, bias, gain, node_small, node_scale = finished(held, (after(small, grad_nodes),))
        for first in (0, middle):
            piece = after(late[plane, first], bias)
            late[plane + ("core",), first] = across(piece, ("core",))
    else:
        for flips in sides[1:]:
            held[flips, 0] = across(own, flips)
        late = {
            (flips + ("core",), first): across(piece, ("core",))
            for (flips, first), piece in held.items()
        }
        *grads, bias, gain, node_small, node_scale = finished(held, (small,))
    grads = finished(late, grads)
    return (
        node_out,
        edge_out,
        grad_nodes,
        edge_grad,
        grads[0],
        bias,
        grads[1],
        gain,
        grads[2],
        node_small,
        grads[3],
        node_scale,
    )


def solution(mesh):
    bands, tiles = mesh.devices.shape
    x_axes = tuple(f"x{bit}" for bit in range((bands // 2).bit_length() - 1))
    y_axes = tuple(f"y{bit}" for bit in range((tiles.bit_length() - 1) // 2))
    names = (*x_axes, "core", "z", *y_axes)
    shape = (2,) * len(x_axes) + (2, tiles // 2 ** len(y_axes)) + (2,) * len(y_axes)
    cores = jax.sharding.Mesh(mesh.devices.reshape(shape), names)
    spread = P(names, None)
    line = P(names)
    cube = P(names, None, None)
    return jax.shard_map(
        partial(shards, x_axes, y_axes),
        mesh=cores,
        in_specs=(spread, spread, line, line, line, cube, cube) + (P(),) * 8 + (spread, spread),
        out_specs=(spread, spread, spread, spread) + (P(),) * 8,
        check_vma=False,
    )
```

time: 336 us -> 148 us (0.44)
  local copies, waits for them, and re-layouts: 82.2 us -> 5.71 us
  other arithmetic: 71.1 us -> 0 us
  Pallas kernels: 0 us -> 48.9 us
  blocking collectives: 40.3 us -> 0 us
  matrix products: 32.6 us -> 0 us
  waiting for transfers between devices: 64 us -> 38.9 us
  starting transfers between devices: 28.6 us -> 52.2 us
  between operations: 15.3 us -> 1.77 us
    psum x1 -> x0, waiting for transfers between devices: 64 us -> none  [shards(): summed = lax.psum(every_grad, ('lat', 'lon'))]
    scatter-add x8 -> x0, other arithmetic: 50.3 us -> none  [the longest x1 15.2 us: shards(): jax.ops.segment_sum(message, receiver, node_rows, indices_are_sorted=True)]
    pallas_call x0 -> x9, Pallas kernels: none -> 48.9 us  [the longest x1 26.3 us: shards(): pl.pallas_call(partial(passes_kernel, peers, capacity, node_rows + rims,...]
    gather x9 -> x0, local copies, waits for them, and re-layouts: 40.9 us -> none  [the longest x2 14.3 us: shards(): from_gathered.astype(jnp.float32)[receiver]]
    psum x1 -> x0, blocking collectives: 40.3 us -> none  [shards(): summed = lax.psum(every_grad, ('lat', 'lon'))]
    ppermute x8 -> x31, waiting for transfers between devices: 0.02 us -> 38.9 us  [the longest x8 15.4 us: swap(): return lax.ppermute(array, axes, pairs)]
    dot_general x12 -> x0, matrix products: 32.6 us -> none  [the longest x3 17.6 us: edge_update(): jnp.dot(joined, weight_in, preferred_element_type=jnp.float32) + bias_in]
    unnamed x87 -> x68, local copies, waits for them, and re-layouts: 32.3 us -> 5.71 us
  transfers between devices with their start and end apart: 11 -> 33, of which waited for: 1 -> 13; matrix products, arithmetic and copies ran while one was open for 25% -> 0% of each run, Pallas kernels for 0% -> 5%
where the time goes in v1:
time: 148 us; the launch traced here: 147 us
  starting transfers between devices  52.2 us (35%)
  Pallas kernels  48.9 us (33%)
  waiting for transfers between devices  38.9 us (26%)
  local copies, waits for them, and re-layouts  5.71 us (4%)
  between operations  1.77 us (1%)
    pallas_call x1, Pallas kernels, shards(): pl.pallas_call(partial(passes_kernel, peers, capacity, node_rows + rims,...  26.3 us
    ppermute x8, waiting for transfers between devices, swap(): return lax.ppermute(array, axes, pairs)  15.4 us
    pallas_call x6, Pallas kernels, call(): pl.pallas_call(kernel, out_shape=out_shape, scratch_shapes=scratch, compi...  14.8 us
    ppermute x17, starting transfers between devices, across(): return lax.ppermute(array, axes, [(i, last - i) for i in range(last + 1)])  13.6 us
    all_to_all x2, starting transfers between devices, exchanged(): lax.all_to_all(parts, everyone, split_axis=0, concat_axis=0, tiled=True)  12.4 us
    ppermute x8, starting transfers between devices, swap(): return lax.ppermute(array, axes, pairs)  12.3 us
    ppermute x17, waiting for transfers between devices, across(): return lax.ppermute(array, axes, [(i, last - i) for i in range(last + 1)])  11.6 us
    ppermute x3, starting transfers between devices, shards(): lax.ppermute(piece, 'z', [(i, i ^ bit) for i in range(depth)])  10 us
  transfers between devices with their start and end apart: 33, of which 13 were waited for; matrix products, arithmetic and copies ran while one was open for 0% of the time, Pallas kernels for 5%

profile of v1, /device:TPU:0, one launch (start us, length us, event | category | flops | bytes accessed | tf_op | source)
XLA Modules:
  0.0 147.5 jit_solution(15197857050887414875)
XLA Ops:
  0.6 2.1 %pick.1 = (f32[256,128]{1,0:T(8,128)}, bf16[32,512]{1,0:T(8,128)(2,1)}, bf16[32,512]{1,0:T(8,128)(2,1)}, bf16[32,512]{1,0:T(8,128)(2,1)}, bf16[32,512]{1,0:T(8,128)(2,1)}) custom-call(s32[1,4,32]{2,1,0:T(4,128)} %halo_ref.2, s32[1,2,32]{2,1,0:T(2,128)} %bitcast.14, bf16[256,512]{1,0:T(8,128)(2,1)} %refs_5_.1), custom_call_target="tpu_custom_call" | custom-call | tf_op jit(solution)/shard_map/pick/pallas_call | solution.py:698
  2.7 7.3 %all-to-all-start = ((f32[32,8,128]{2,1,0:T(8,128)}), f32[32,8,128]{2,1,0:T(8,128)S(1)}, u32[]{:S(2)}, u32[]{:S(2)}) async-start(f32[32,8,128]{2,1,0:T(8,128)} %bitcast.13), calls=%async_computation | async-start | bytes 262144 | tf_op jit(solution)/shard_map/all_to_all | solution.py:693
  10.3 0.7 collective-permute-start.1
  11.0 1.7 %collective-permute-start.2 = (bf16[32,512]{1,0:T(8,128)(2,1)}, bf16[32,512]{1,0:T(8,128)(2,1)S(1)}, u32[]{:S(2)}, u32[]{:S(2)}) collective-permute-start(bf16[32,512]{1,0:T(8,128)(2,1)} %get-tuple-element.75), channel_id=1, source_target_pairs={{0,1},{1,0},{2,3},{3,2},{4,5},{5,4},{6,7},{7,6},{8,9},{9,8},{10,11... | collective-permute-start | bytes 98312 | tf_op jit(solution)/shard_map/ppermute | solution.py:638
  12.7 3.3 %collective-permute-start.3 = (bf16[32,512]{1,0:T(8,128)(2,1)}, bf16[32,512]{1,0:T(8,128)(2,1)S(1)}, u32[]{:S(2)}, u32[]{:S(2)}) collective-permute-start(bf16[32,512]{1,0:T(8,128)(2,1)} %get-tuple-element.76), channel_id=1, source_target_pairs={{1,2},{2,1},{3,4},{4,3},{5,6},{6,5},{7,0},{0,7},{9,10},{10,9},{11,... | collective-permute-start | bytes 98312 | tf_op jit(solution)/shard_map/ppermute | solution.py:638
  16.8 2.8 %collective-permute-done.3.refs_9_ = bf16[32,512]{1,0:T(8,128)(2,1)S(1)} collective-permute-done((bf16[32,512]{1,0:T(8,128)(2,1)}, bf16[32,512]{1,0:T(8,128)(2,1)S(1)}, u32[]{:S(2)}, u32[]{:S(2)}) %collective-permute-start.3) | collective-permute-done | bytes 32800 | tf_op jit(solution)/shard_map/ppermute | solution.py:638
  19.6 0.6 copy-done.33
  20.2 26.3 %passes.1 = (bf16[2048,512]{1,0:T(8,128)(2,1)}, bf16[2048,512]{1,0:T(8,128)(2,1)}, bf16[256,512]{1,0:T(8,128)(2,1)}, f32[256,512]{1,0:T(8,128)}, f32[256,128]{1,...) custom-call(s32[1]{0:T(128)S(6)} %copy.37.refs_0_, ...), custom_call_target="tpu_custom_call" | custom-call | flops 20000000000 | bytes 20000000 | tf_op jit(solution)/shard_map/passes/pallas_call | solution.py:756
  46.6 1.5 %collective-permute-start.4 = (bf16[1824,512]{1,0:T(8,128)(2,1)}, bf16[1824,512]{1,0:T(8,128)(2,1)S(1)}, u32[]{:S(2)}, u32[]{:S(2)}) collective-permute-start(bf16[1824,512]{1,0:T(8,128)(2,1)} %get-tuple-element.87), channel_id=1, source_target_pairs={{0,8},{8,0},{1,9},{9,1},{2,10},{10,2},{3,11},{11,3},{4,12},{12,4},... | collective-permute-start | bytes 5603336 | tf_op jit(solution)/shard_map/ppermute | solution.py:714
  48.1 3.7 %collective-permute-done.4.got = bf16[1824,512]{1,0:T(8,128)(2,1)S(1)} collective-permute-done((bf16[1824,512]{1,0:T(8,128)(2,1)}, bf16[1824,512]{1,0:T(8,128)(2,1)S(1)}, u32[]{:S(2)}, u32[]{:S(2)}) %collective-permute-start.4) | collective-permute-done | bytes 1867808 | tf_op jit(solution)/shard_map/ppermute | solution.py:714
  51.7 1.2 copy-done
  53.0 3.7 %plane.1 = (bf16[464,512]{1,0:T(8,128)(2,1)}, bf16[464,512]{1,0:T(8,128)(2,1)}, bf16[464,512]{1,0:T(8,128)(2,1)}, bf16[464,512]{1,0:T(8,128)(2,1)}) custom-call(bf16[1824,512]{1,0:T(8,128)(2,1)} %get-tuple-element.86.keep, bf16[1824,512]{1,0:T(8,128)(2,1)} %copy-done), custom_call_target="tpu_custom_call" | custom-call | tf_op jit(solution)/shard_map/plane/pallas_call | solution.py:698
  56.7 2.2 %collective-permute-start.9 = (bf16[464,512]{1,0:T(8,128)(2,1)}, bf16[464,512]{1,0:T(8,128)(2,1)S(1)}, u32[]{:S(2)}, u32[]{:S(2)}) collective-permute-start(bf16[464,512]{1,0:T(8,128)(2,1)} %get-tuple-element.89), channel_id=1, source_target_pairs={{0,16},{16,0},{1,17},{17,1},{2,18},{18,2},{3,19},{19,3},{4,20},{20... | collective-permute-start | bytes 1425416 | tf_op jit(solution)/shard_map/ppermute | solution.py:714
  58.8 1.5 collective-permute-start.11
  60.3 5.1 %all-to-all-start.1 = ((f32[32,8,128]{2,1,0:T(8,128)}), f32[32,8,128]{2,1,0:T(8,128)S(1)}, u32[]{:S(2)}, u32[]{:S(2)}) async-start(f32[32,8,128]{2,1,0:T(8,128)} %bitcast.9), calls=%async_computation.1 | async-start | bytes 262144 | tf_op jit(solution)/shard_map/all_to_all | solution.py:693
  65.8 0.8 collective-permute-start.6
  66.7 1.8 %collective-permute-start.7 = (bf16[32,512]{1,0:T(8,128)(2,1)S(1)}, bf16[32,512]{1,0:T(8,128)(2,1)S(1)}, u32[]{:S(2)}, u32[]{:S(2)}) collective-permute-start(bf16[32,512]{1,0:T(8,128)(2,1)S(1)} %copy-done.27), channel_id=1, source_target_pairs={{0,1},{1,0},{2,3},{3,2},{4,5},{5,4},{6,7},{7,6},{8,9},{9,8},{10,11... | collective-permute-start | bytes 98312 | tf_op jit(solution)/shard_map/ppermute | solution.py:638
  68.5 3.4 %collective-permute-start.8 = (bf16[32,512]{1,0:T(8,128)(2,1)S(1)}, bf16[32,512]{1,0:T(8,128)(2,1)S(1)}, u32[]{:S(2)}, u32[]{:S(2)}) collective-permute-start(bf16[32,512]{1,0:T(8,128)(2,1)S(1)} %copy-done.26), channel_id=1, source_target_pairs={{1,2},{2,1},{3,4},{4,3},{5,6},{6,5},{7,0},{0,7},{9,10},{10,9},{11,... | collective-permute-start | bytes 98312 | tf_op jit(solution)/shard_map/ppermute | solution.py:638
  71.9 12.4 %collective-permute-done.7.refs_2_ = bf16[32,512]{1,0:T(8,128)(2,1)S(1)} collective-permute-done((bf16[32,512]{1,0:T(8,128)(2,1)S(1)}, bf16[32,512]{1,0:T(8,128)(2,1)S(1)}, u32[]{:S(2)}, u32[]{:S(2)}) %collective-permute-start.7) | collective-permute-done | bytes 32800 | tf_op jit(solution)/shard_map/ppermute | solution.py:638
  84.4 0.7 copy-done.2
  85.5 2.7 %line.1 = (bf16[128,512]{1,0:T(8,128)(2,1)}, bf16[128,512]{1,0:T(8,128)(2,1)}, bf16[128,512]{1,0:T(8,128)(2,1)}, bf16[128,512]{1,0:T(8,128)(2,1)}) custom-call(bf16[464,512]{1,0:T(8,128)(2,1)} %get-tuple-element.97.refs_0_, bf16[464,512]{1,0:T(8,128)(2,1)} %copy-done.2, bf16[464,512]{1,0:T(8,128)(2,1)} %copy-done.3, bf16[464,512]{1,0:T(8,128)(2,1)} %copy-done.4), custom_call_target="tpu_custom_call" | custom-call | tf_op jit(solution)/shard_map/line/pallas_call | solution.py:698
  88.2 2.7 %collective-permute-start.13 = (bf16[128,512]{1,0:T(8,128)(2,1)}, bf16[128,512]{1,0:T(8,128)(2,1)S(1)}, u32[]{:S(2)}, u32[]{:S(2)}) collective-permute-start(bf16[128,512]{1,0:T(8,128)(2,1)} %get-tuple-element.103), channel_id=1, source_target_pairs={{0,4},{2,6},{4,0},{6,2},{1,5},{3,7},{5,1},{7,3},{8,12},{10,14},{12... | collective-permute-start | bytes 393224 | tf_op jit(solution)/shard_map/ppermute | solution.py:718
  90.9 1.1 collective-permute-start.14
  92.0 3.3 %collective-permute-done.12.refs_1_ = bf16[128,512]{1,0:T(8,128)(2,1)S(1)} collective-permute-done((bf16[128,512]{1,0:T(8,128)(2,1)}, bf16[128,512]{1,0:T(8,128)(2,1)S(1)}, u32[]{:S(2)}, u32[]{:S(2)}) %collective-permute-start.12) | collective-permute-done | bytes 131104 | tf_op jit(solution)/shard_map/ppermute | solution.py:718
  95.3 3.2 %collective-permute-done.13.refs_2_ = bf16[128,512]{1,0:T(8,128)(2,1)S(1)} collective-permute-done((bf16[128,512]{1,0:T(8,128)(2,1)}, bf16[128,512]{1,0:T(8,128)(2,1)S(1)}, u32[]{:S(2)}, u32[]{:S(2)}) %collective-permute-start.13) | collective-permute-done | bytes 131104 | tf_op jit(solution)/shard_map/ppermute | solution.py:718
  98.5 0.6 copy-done.17
  99.2 1.8 %total.1 = (bf16[112,512]{1,0:T(8,128)(2,1)}, f32[16,512]{1,0:T(8,128)}) custom-call(bf16[128,512]{1,0:T(8,128)(2,1)} %get-tuple-element.101.refs_0_, bf16[128,512]{1,0:T(8,128)(2,1)} %copy-done.16, bf16[128,512]{1,0:T(8,128)(2,1)} %copy-done.17, bf16[128,512]{1,0:T(8,128)(2,1)} %copy-done.18), custom_call_target="tpu_custom_call" | custom-call | tf_op jit(solution)/shard_map/total/pallas_call | solution.py:698
  101.0 4.2 %collective-permute-start.16 = (bf16[112,512]{1,0:T(8,128)(2,1)}, bf16[112,512]{1,0:T(8,128)(2,1)S(1)}, u32[]{:S(2)}, u32[]{:S(2)}) collective-permute-start(bf16[112,512]{1,0:T(8,128)(2,1)} %get-tuple-element.105.refs_0_), channel_id=1, source_target_pairs={{0,4},{2,6},{4,0},{6,2},{1,5},{3,7},{5,1},{7,3},{8,12},{10,14},{12... | collective-permute-start | bytes 344072 | tf_op jit(solution)/shard_map/ppermute | solution.py:848
  105.2 1.5 %collective-permute-start.15 = (bf16[112,512]{1,0:T(8,128)(2,1)}, bf16[112,512]{1,0:T(8,128)(2,1)S(1)}, u32[]{:S(2)}, u32[]{:S(2)}) collective-permute-start(bf16[112,512]{1,0:T(8,128)(2,1)} %get-tuple-element.105.refs_0_), channel_id=1, source_target_pairs={{0,2},{2,0},{4,6},{6,4},{1,3},{3,1},{5,7},{7,5},{8,10},{10,8},{12,... | collective-permute-start | bytes 344072 | tf_op jit(solution)/shard_map/ppermute | solution.py:848
  106.7 2.2 %collective-permute-done.16.refs_2_ = bf16[112,512]{1,0:T(8,128)(2,1)S(1)} collective-permute-done((bf16[112,512]{1,0:T(8,128)(2,1)}, bf16[112,512]{1,0:T(8,128)(2,1)S(1)}, u32[]{:S(2)}, u32[]{:S(2)}) %collective-permute-start.16) | collective-permute-done | bytes 114720 | tf_op jit(solution)/shard_map/ppermute | solution.py:848
  108.9 4.3 %collective-permute-start.17 = (bf16[112,512]{1,0:T(8,128)(2,1)S(1)}, bf16[112,512]{1,0:T(8,128)(2,1)S(1)}, u32[]{:S(2)}, u32[]{:S(2)}) collective-permute-start(bf16[112,512]{1,0:T(8,128)(2,1)S(1)} %collective-permute-done.16.refs_2_), channel_id=1, source_target_pairs={{0,2},{2,0},{4,6},{6,4},{1,3},{3,1},{5,7},{7,5},{8,10},{10,8},{12,... | collective-permute-start | bytes 344072 | tf_op jit(solution)/shard_map/ppermute | solution.py:848
  113.2 3.2 %collective-permute-done.17.refs_3_ = bf16[112,512]{1,0:T(8,128)(2,1)S(1)} collective-permute-done((bf16[112,512]{1,0:T(8,128)(2,1)S(1)}, bf16[112,512]{1,0:T(8,128)(2,1)S(1)}, u32[]{:S(2)}, u32[]{:S(2)}) %collective-permute-start.17) | collective-permute-done | bytes 114720 | tf_op jit(solution)/shard_map/ppermute | solution.py:848
  116.5 0.6 copy-done.21
  117.1 2.0 %join.1 = (bf16[448,512]{1,0:T(8,128)(2,1)}, bf16[224,512]{1,0:T(8,128)(2,1)}, bf16[224,512]{1,0:T(8,128)(2,1)}) custom-call(bf16[112,512]{1,0:T(8,128)(2,1)} %get-tuple-element.105.refs_0_, bf16[112,512]{1,0:T(8,128)(2,1)} %copy-done.20, bf16[112,512]{1,0:T(8,128)(2,1)} %copy-done.19, bf16[112,512]{1,0:T(8,128)(2,1)} %copy-done.21), custom_call_target="tpu_custom_call" | custom-call | tf_op jit(solution)/shard_map/join/pallas_call | solution.py:698
  119.2 2.0 %collective-permute-start.20 = (bf16[224,512]{1,0:T(8,128)(2,1)}, bf16[224,512]{1,0:T(8,128)(2,1)S(1)}, u32[]{:S(2)}, u32[]{:S(2)}) collective-permute-start(bf16[224,512]{1,0:T(8,128)(2,1)} %get-tuple-element.117), channel_id=1, source_target_pairs={{0,16},{16,0},{1,17},{17,1},{2,18},{18,2},{3,19},{19,3},{4,20},{20... | collective-permute-start | bytes 688136 | tf_op jit(solution)/shard_map/ppermute | solution.py:714
  121.1 1.1 collective-permute-start.18
  122.3 1.0 collective-permute-start.22
  123.3 4.5 %collective-permute-done.20.refs_1_ = bf16[224,512]{1,0:T(8,128)(2,1)S(1)} collective-permute-done((bf16[224,512]{1,0:T(8,128)(2,1)}, bf16[224,512]{1,0:T(8,128)(2,1)S(1)}, u32[]{:S(2)}, u32[]{:S(2)}) %collective-permute-start.20) | collective-permute-done | bytes 229408 | tf_op jit(solution)/shard_map/ppermute | solution.py:714
  127.8 2.0 %collective-permute-start.21 = (bf16[224,512]{1,0:T(8,128)(2,1)S(1)}, bf16[224,512]{1,0:T(8,128)(2,1)S(1)}, u32[]{:S(2)}, u32[]{:S(2)}) collective-permute-start(bf16[224,512]{1,0:T(8,128)(2,1)S(1)} %collective-permute-done.20.refs_1_), channel_id=1, source_target_pairs={{0,1},{1,0},{2,3},{3,2},{4,5},{5,4},{6,7},{7,6},{8,9},{9,8},{10,11... | collective-permute-start | bytes 688136 | tf_op jit(solution)/shard_map/ppermute | solution.py:714
  129.9 1.1 collective-permute-start.19
  130.9 1.8 %collective-permute-done.22.refs_3_ = bf16[224,512]{1,0:T(8,128)(2,1)S(1)} collective-permute-done((bf16[224,512]{1,0:T(8,128)(2,1)}, bf16[224,512]{1,0:T(8,128)(2,1)S(1)}, u32[]{:S(2)}, u32[]{:S(2)}) %collective-permute-start.22) | collective-permute-done | bytes 229408 | tf_op jit(solution)/shard_map/ppermute | solution.py:714
  132.8 2.5 %returned.1 = bf16[256,512]{1,0:T(8,128)(2,1)} custom-call(s32[1,4,32]{2,1,0:T(4,128)} %halo_ref.2, s32[1,2,32]{2,1,0:T(2,128)} %bitcast.15, f32[256,512]{1,0:T(8,128)} %get-tuple-element.109.totals_ref, f32[256,128]{1,0:T(8,128)} %bitcast.11, bf16[32,512]{1,0:T(8,128)(2,1)} %copy-done.22, bf16[32,512]{1,0:T(8,128)(2,1)} %copy-done.23, ...), custom_call_target="tpu_custom_call" | custom-call | tf_op jit(solution)/shard_map/returned/pallas_call | solution.py:698
  135.3 0.5 collective-permute-start.25
  136.0 0.6 copy-done.5
  136.5 4.2 %finish.2 = (f32[1536,512]{1,0:T(8,128)}, f32[512,512]{1,0:T(8,128)}, f32[1024,512]{1,0:T(8,128)}, f32[512,512]{1,0:T(8,128)}, f32[512]{0:T(512)}, /*index=5*/f32[512]{0:T(512)}, f32[512]{0:T(512)}, f32[512]{0:T(512)}) custom-call(bf16[448,512]{1,0:T(8,128)(2,1)} %get-tuple-element.106.refs_0_, bf16[224,512]{1,0:T(8,128)(2,1)} %copy-done.6, ...), custom_call_target="tpu_custom_call" | custom-call | tf_op jit(solution)/shard_map/finish/pallas_call | solution.py:872
  140.9 0.4 collective-permute-start.29
  141.4 1.1 collective-permute-done.24.refs_3_
  143.6 3.7 %finish.3 = (f32[1536,512]{1,0:T(8,128)}, f32[512,512]{1,0:T(8,128)}, f32[1024,512]{1,0:T(8,128)}, f32[512,512]{1,0:T(8,128)}) custom-call(bf16[224,512]{1,0:T(8,128)(2,1)} %copy-done.11, bf16[224,512]{1,0:T(8,128)(2,1)} %copy-done.10, ...), custom_call_target="tpu_custom_call", output_to_operand_aliasing={{0}: (8, {}), {1}: (9, {}), {2}: (10, {}), {3}: (11, {})} | custom-call | tf_op jit(solution)/shard_map/finish/pallas_call | solution.py:872
  (95 shorter events, 2.9 us)
Async XLA Ops:
  2.7 16.8 %all-to-all-start = ((f32[32,8,128]{2,1,0:T(8,128)}), f32[32,8,128]{2,1,0:T(8,128)S(1)}, u32[]{:S(2)}, u32[]{:S(2)}) async-start(f32[32,8,128]{2,1,0:T(8,128)} %bitcast.13), calls=%async_computation | async-start | bytes 262144 | tf_op jit(solution)/shard_map/all_to_all | solution.py:693
  10.0 6.7 %collective-permute-start = (bf16[32,512]{1,0:T(8,128)(2,1)}, bf16[32,512]{1,0:T(8,128)(2,1)S(1)}, u32[]{:S(2)}, u32[]{:S(2)}) collective-permute-start(bf16[32,512]{1,0:T(8,128)(2,1)} %get-tuple-element.73), channel_id=1, source_target_pairs={{0,8},{8,0},{16,24},{24,16},{1,9},{9,1},{17,25},{25,17},{2,10},{10... | collective-permute-start | bytes 98312 | tf_op jit(solution)/shard_map/ppermute | solution.py:638
  10.3 6.4 %collective-permute-start.1 = (bf16[32,512]{1,0:T(8,128)(2,1)}, bf16[32,512]{1,0:T(8,128)(2,1)S(1)}, u32[]{:S(2)}, u32[]{:S(2)}) collective-permute-start(bf16[32,512]{1,0:T(8,128)(2,1)} %get-tuple-element.74), channel_id=1, source_target_pairs={{8,16},{16,8},{9,17},{17,9},{10,18},{18,10},{11,19},{19,11},{12,20... | collective-permute-start | bytes 98312 | tf_op jit(solution)/shard_map/ppermute | solution.py:638
  11.0 5.7 %collective-permute-start.2 = (bf16[32,512]{1,0:T(8,128)(2,1)}, bf16[32,512]{1,0:T(8,128)(2,1)S(1)}, u32[]{:S(2)}, u32[]{:S(2)}) collective-permute-start(bf16[32,512]{1,0:T(8,128)(2,1)} %get-tuple-element.75), channel_id=1, source_target_pairs={{0,1},{1,0},{2,3},{3,2},{4,5},{5,4},{6,7},{7,6},{8,9},{9,8},{10,11... | collective-permute-start | bytes 98312 | tf_op jit(solution)/shard_map/ppermute | solution.py:638
  12.7 6.8 %collective-permute-start.3 = (bf16[32,512]{1,0:T(8,128)(2,1)}, bf16[32,512]{1,0:T(8,128)(2,1)S(1)}, u32[]{:S(2)}, u32[]{:S(2)}) collective-permute-start(bf16[32,512]{1,0:T(8,128)(2,1)} %get-tuple-element.76), channel_id=1, source_target_pairs={{1,2},{2,1},{3,4},{4,3},{5,6},{6,5},{7,0},{0,7},{9,10},{10,9},{11,... | collective-permute-start | bytes 98312 | tf_op jit(solution)/shard_map/ppermute | solution.py:638
  46.5 18.9 %copy-start.29 = (bf16[32,512]{1,0:T(8,128)(2,1)S(1)}, bf16[32,512]{1,0:T(8,128)(2,1)}, u32[]{:S(2)}) copy-start(bf16[32,512]{1,0:T(8,128)(2,1)} %get-tuple-element.93) | copy-start | bytes 98308
  46.5 19.2 %copy-start.28 = (bf16[32,512]{1,0:T(8,128)(2,1)S(1)}, bf16[32,512]{1,0:T(8,128)(2,1)}, u32[]{:S(2)}) copy-start(bf16[32,512]{1,0:T(8,128)(2,1)} %get-tuple-element.94) | copy-start | bytes 98308
  46.5 20.2 %copy-start.27 = (bf16[32,512]{1,0:T(8,128)(2,1)S(1)}, bf16[32,512]{1,0:T(8,128)(2,1)}, u32[]{:S(2)}) copy-start(bf16[32,512]{1,0:T(8,128)(2,1)} %get-tuple-element.95) | copy-start | bytes 98308
  46.6 22.0 %copy-start.26 = (bf16[32,512]{1,0:T(8,128)(2,1)S(1)}, bf16[32,512]{1,0:T(8,128)(2,1)}, u32[]{:S(2)}) copy-start(bf16[32,512]{1,0:T(8,128)(2,1)} %get-tuple-element.96) | copy-start | bytes 98308
  46.6 5.2 %collective-permute-start.4 = (bf16[1824,512]{1,0:T(8,128)(2,1)}, bf16[1824,512]{1,0:T(8,128)(2,1)S(1)}, u32[]{:S(2)}, u32[]{:S(2)}) collective-permute-start(bf16[1824,512]{1,0:T(8,128)(2,1)} %get-tuple-element.87), channel_id=1, source_target_pairs={{0,8},{8,0},{1,9},{9,1},{2,10},{10,2},{3,11},{11,3},{4,12},{12,4},... | collective-permute-start | bytes 5603336 | tf_op jit(solution)/shard_map/ppermute | solution.py:714
  56.7 27.7 %collective-permute-start.9 = (bf16[464,512]{1,0:T(8,128)(2,1)}, bf16[464,512]{1,0:T(8,128)(2,1)S(1)}, u32[]{:S(2)}, u32[]{:S(2)}) collective-permute-start(bf16[464,512]{1,0:T(8,128)(2,1)} %get-tuple-element.89), channel_id=1, source_target_pairs={{0,16},{16,0},{1,17},{17,1},{2,18},{18,2},{3,19},{19,3},{4,20},{20... | collective-permute-start | bytes 1425416 | tf_op jit(solution)/shard_map/ppermute | solution.py:714
  58.8 25.5 %collective-permute-start.10 = (bf16[464,512]{1,0:T(8,128)(2,1)}, bf16[464,512]{1,0:T(8,128)(2,1)S(1)}, u32[]{:S(2)}, u32[]{:S(2)}) collective-permute-start(bf16[464,512]{1,0:T(8,128)(2,1)} %get-tuple-element.90), channel_id=1, source_target_pairs={{0,1},{1,0},{2,3},{3,2},{4,5},{5,4},{6,7},{7,6},{8,9},{9,8},{10,11... | collective-permute-start | bytes 1425416 | tf_op jit(solution)/shard_map/ppermute | solution.py:714
  58.8 25.6 %collective-permute-start.11 = (bf16[464,512]{1,0:T(8,128)(2,1)}, bf16[464,512]{1,0:T(8,128)(2,1)S(1)}, u32[]{:S(2)}, u32[]{:S(2)}) collective-permute-start(bf16[464,512]{1,0:T(8,128)(2,1)} %get-tuple-element.91), channel_id=1, source_target_pairs={{0,17},{1,16},{16,1},{17,0},{2,19},{3,18},{18,3},{19,2},{4,21},{5,... | collective-permute-start | bytes 1425416 | tf_op jit(solution)/shard_map/ppermute | solution.py:714
  60.3 24.0 %all-to-all-start.1 = ((f32[32,8,128]{2,1,0:T(8,128)}), f32[32,8,128]{2,1,0:T(8,128)S(1)}, u32[]{:S(2)}, u32[]{:S(2)}) async-start(f32[32,8,128]{2,1,0:T(8,128)} %bitcast.9), calls=%async_computation.1 | async-start | bytes 262144 | tf_op jit(solution)/shard_map/all_to_all | solution.py:693
  65.5 1.3 collective-permute-start.5
  65.8 2.7 %collective-permute-start.6 = (bf16[32,512]{1,0:T(8,128)(2,1)S(1)}, bf16[32,512]{1,0:T(8,128)(2,1)S(1)}, u32[]{:S(2)}, u32[]{:S(2)}) collective-permute-start(bf16[32,512]{1,0:T(8,128)(2,1)S(1)} %copy-done.28), channel_id=1, source_target_pairs={{8,16},{16,8},{9,17},{17,9},{10,18},{18,10},{11,19},{19,11},{12,20... | collective-permute-start | bytes 98312 | tf_op jit(solution)/shard_map/ppermute | solution.py:638
  66.7 66.0 %copy-start.22 = (bf16[32,512]{1,0:T(8,128)(2,1)}, bf16[32,512]{1,0:T(8,128)(2,1)S(1)}, u32[]{:S(2)}) copy-start(bf16[32,512]{1,0:T(8,128)(2,1)S(1)} %collective-permute-done.5.refs_0_) | copy-start | bytes 98308
  66.7 17.6 %collective-permute-start.7 = (bf16[32,512]{1,0:T(8,128)(2,1)S(1)}, bf16[32,512]{1,0:T(8,128)(2,1)S(1)}, u32[]{:S(2)}, u32[]{:S(2)}) collective-permute-start(bf16[32,512]{1,0:T(8,128)(2,1)S(1)} %copy-done.27), channel_id=1, source_target_pairs={{0,1},{1,0},{2,3},{3,2},{4,5},{5,4},{6,7},{7,6},{8,9},{9,8},{10,11... | collective-permute-start | bytes 98312 | tf_op jit(solution)/shard_map/ppermute | solution.py:638
  68.5 64.3 %copy-start.23 = (bf16[32,512]{1,0:T(8,128)(2,1)}, bf16[32,512]{1,0:T(8,128)(2,1)S(1)}, u32[]{:S(2)}) copy-start(bf16[32,512]{1,0:T(8,128)(2,1)S(1)} %collective-permute-done.6.refs_1_) | copy-start | bytes 98308
  68.5 15.8 %collective-permute-start.8 = (bf16[32,512]{1,0:T(8,128)(2,1)S(1)}, bf16[32,512]{1,0:T(8,128)(2,1)S(1)}, u32[]{:S(2)}, u32[]{:S(2)}) collective-permute-start(bf16[32,512]{1,0:T(8,128)(2,1)S(1)} %copy-done.26), channel_id=1, source_target_pairs={{1,2},{2,1},{3,4},{4,3},{5,6},{6,5},{7,0},{0,7},{9,10},{10,9},{11,... | collective-permute-start | bytes 98312 | tf_op jit(solution)/shard_map/ppermute | solution.py:638
  84.3 34.8 %copy-start.24 = (bf16[32,512]{1,0:T(8,128)(2,1)}, bf16[32,512]{1,0:T(8,128)(2,1)S(1)}, u32[]{:S(2)}) copy-start(bf16[32,512]{1,0:T(8,128)(2,1)S(1)} %collective-permute-done.7.refs_2_) | copy-start | bytes 98308
  84.3 34.8 %copy-start.25 = (bf16[32,512]{1,0:T(8,128)(2,1)}, bf16[32,512]{1,0:T(8,128)(2,1)S(1)}, u32[]{:S(2)}) copy-start(bf16[32,512]{1,0:T(8,128)(2,1)S(1)} %collective-permute-done.8.refs_3_) | copy-start | bytes 98308
  84.3 48.4 %copy-start.1 = (f32[32,8,128]{2,1,0:T(8,128)}, f32[32,8,128]{2,1,0:T(8,128)S(1)}, u32[]{:S(2)}) copy-start(f32[32,8,128]{2,1,0:T(8,128)S(1)} %all-to-all-done.1) | copy-start | bytes 393220
  88.2 7.1 %collective-permute-start.12 = (bf16[128,512]{1,0:T(8,128)(2,1)}, bf16[128,512]{1,0:T(8,128)(2,1)S(1)}, u32[]{:S(2)}, u32[]{:S(2)}) collective-permute-start(bf16[128,512]{1,0:T(8,128)(2,1)} %get-tuple-element.102), channel_id=1, source_target_pairs={{0,2},{2,4},{4,6},{6,0},{1,3},{3,5},{5,7},{7,1},{8,10},{10,12},{12... | collective-permute-start | bytes 393224 | tf_op jit(solution)/shard_map/ppermute | solution.py:718
  88.2 10.3 %collective-permute-start.13 = (bf16[128,512]{1,0:T(8,128)(2,1)}, bf16[128,512]{1,0:T(8,128)(2,1)S(1)}, u32[]{:S(2)}, u32[]{:S(2)}) collective-permute-start(bf16[128,512]{1,0:T(8,128)(2,1)} %get-tuple-element.103), channel_id=1, source_target_pairs={{0,4},{2,6},{4,0},{6,2},{1,5},{3,7},{5,1},{7,3},{8,12},{10,14},{12... | collective-permute-start | bytes 393224 | tf_op jit(solution)/shard_map/ppermute | solution.py:718
  90.9 7.6 %collective-permute-start.14 = (bf16[128,512]{1,0:T(8,128)(2,1)}, bf16[128,512]{1,0:T(8,128)(2,1)S(1)}, u32[]{:S(2)}, u32[]{:S(2)}) collective-permute-start(bf16[128,512]{1,0:T(8,128)(2,1)} %get-tuple-element.104), channel_id=1, source_target_pairs={{0,6},{2,0},{4,2},{6,4},{1,7},{3,1},{5,3},{7,5},{8,14},{10,8},{12,... | collective-permute-start | bytes 393224 | tf_op jit(solution)/shard_map/ppermute | solution.py:718
  95.3 3.2 %copy-start.16 = (bf16[128,512]{1,0:T(8,128)(2,1)}, bf16[128,512]{1,0:T(8,128)(2,1)S(1)}, u32[]{:S(2)}) copy-start(bf16[128,512]{1,0:T(8,128)(2,1)S(1)} %collective-permute-done.12.refs_1_) | copy-start | bytes 393220
  101.0 7.9 %collective-permute-start.16 = (bf16[112,512]{1,0:T(8,128)(2,1)}, bf16[112,512]{1,0:T(8,128)(2,1)S(1)}, u32[]{:S(2)}, u32[]{:S(2)}) collective-permute-start(bf16[112,512]{1,0:T(8,128)(2,1)} %get-tuple-element.105.refs_0_), channel_id=1, source_target_pairs={{0,4},{2,6},{4,0},{6,2},{1,5},{3,7},{5,1},{7,3},{8,12},{10,14},{12... | collective-permute-start | bytes 344072 | tf_op jit(solution)/shard_map/ppermute | solution.py:848
  105.2 8.0 %collective-permute-start.15 = (bf16[112,512]{1,0:T(8,128)(2,1)}, bf16[112,512]{1,0:T(8,128)(2,1)S(1)}, u32[]{:S(2)}, u32[]{:S(2)}) collective-permute-start(bf16[112,512]{1,0:T(8,128)(2,1)} %get-tuple-element.105.refs_0_), channel_id=1, source_target_pairs={{0,2},{2,0},{4,6},{6,4},{1,3},{3,1},{5,7},{7,5},{8,10},{10,8},{12,... | collective-permute-start | bytes 344072 | tf_op jit(solution)/shard_map/ppermute | solution.py:848
  108.9 7.6 %copy-start.19 = (bf16[112,512]{1,0:T(8,128)(2,1)}, bf16[112,512]{1,0:T(8,128)(2,1)S(1)}, u32[]{:S(2)}) copy-start(bf16[112,512]{1,0:T(8,128)(2,1)S(1)} %collective-permute-done.16.refs_2_) | copy-start | bytes 344068
  108.9 7.6 %collective-permute-start.17 = (bf16[112,512]{1,0:T(8,128)(2,1)S(1)}, bf16[112,512]{1,0:T(8,128)(2,1)S(1)}, u32[]{:S(2)}, u32[]{:S(2)}) collective-permute-start(bf16[112,512]{1,0:T(8,128)(2,1)S(1)} %collective-permute-done.16.refs_2_), channel_id=1, source_target_pairs={{0,2},{2,0},{4,6},{6,4},{1,3},{3,1},{5,7},{7,5},{8,10},{10,8},{12,... | collective-permute-start | bytes 344072 | tf_op jit(solution)/shard_map/ppermute | solution.py:848
  113.2 3.2 %copy-start.20 = (bf16[112,512]{1,0:T(8,128)(2,1)}, bf16[112,512]{1,0:T(8,128)(2,1)S(1)}, u32[]{:S(2)}) copy-start(bf16[112,512]{1,0:T(8,128)(2,1)S(1)} %collective-permute-done.15.refs_1_) | copy-start | bytes 344068
  119.1 16.6 %collective-permute-start.28 = (bf16[448,512]{1,0:T(8,128)(2,1)}, bf16[448,512]{1,0:T(8,128)(2,1)S(1)}, u32[]{:S(2)}, u32[]{:S(2)}) collective-permute-start(bf16[448,512]{1,0:T(8,128)(2,1)} %get-tuple-element.106.refs_0_), channel_id=1, source_target_pairs={{0,8},{8,0},{1,9},{9,1},{2,10},{10,2},{3,11},{11,3},{4,12},{12,4},... | collective-permute-start | bytes 1376264 | tf_op jit(solution)/shard_map/ppermute | solution.py:714
  119.2 8.7 %collective-permute-start.20 = (bf16[224,512]{1,0:T(8,128)(2,1)}, bf16[224,512]{1,0:T(8,128)(2,1)S(1)}, u32[]{:S(2)}, u32[]{:S(2)}) collective-permute-start(bf16[224,512]{1,0:T(8,128)(2,1)} %get-tuple-element.117), channel_id=1, source_target_pairs={{0,16},{16,0},{1,17},{17,1},{2,18},{18,2},{3,19},{19,3},{4,20},{20... | collective-permute-start | bytes 688136 | tf_op jit(solution)/shard_map/ppermute | solution.py:714
  121.1 8.7 %collective-permute-start.18 = (bf16[224,512]{1,0:T(8,128)(2,1)}, bf16[224,512]{1,0:T(8,128)(2,1)S(1)}, u32[]{:S(2)}, u32[]{:S(2)}) collective-permute-start(bf16[224,512]{1,0:T(8,128)(2,1)} %get-tuple-element.116), channel_id=1, source_target_pairs={{0,1},{1,0},{2,3},{3,2},{4,5},{5,4},{6,7},{7,6},{8,9},{9,8},{10,11... | collective-permute-start | bytes 688136 | tf_op jit(solution)/shard_map/ppermute | solution.py:714
  122.3 10.5 %collective-permute-start.22 = (bf16[224,512]{1,0:T(8,128)(2,1)}, bf16[224,512]{1,0:T(8,128)(2,1)S(1)}, u32[]{:S(2)}, u32[]{:S(2)}) collective-permute-start(bf16[224,512]{1,0:T(8,128)(2,1)} %get-tuple-element.116), channel_id=1, source_target_pairs={{0,16},{16,0},{1,17},{17,1},{2,18},{18,2},{3,19},{19,3},{4,20},{20... | collective-permute-start | bytes 688136 | tf_op jit(solution)/shard_map/ppermute | solution.py:714
  123.3 12.0 %collective-permute-start.26 = (bf16[224,512]{1,0:T(8,128)(2,1)}, bf16[224,512]{1,0:T(8,128)(2,1)S(1)}, u32[]{:S(2)}, u32[]{:S(2)}) collective-permute-start(bf16[224,512]{1,0:T(8,128)(2,1)} %get-tuple-element.117), channel_id=1, source_target_pairs={{0,1},{1,0},{2,3},{3,2},{4,5},{5,4},{6,7},{7,6},{8,9},{9,8},{10,11... | collective-permute-start | bytes 688136 | tf_op jit(solution)/shard_map/ppermute | solution.py:714
  127.8 8.0 %copy-start.6 = (bf16[224,512]{1,0:T(8,128)(2,1)}, bf16[224,512]{1,0:T(8,128)(2,1)S(1)}, u32[]{:S(2)}) copy-start(bf16[224,512]{1,0:T(8,128)(2,1)S(1)} %collective-permute-done.20.refs_1_) | copy-start | bytes 688132
  127.8 12.9 %collective-permute-start.21 = (bf16[224,512]{1,0:T(8,128)(2,1)S(1)}, bf16[224,512]{1,0:T(8,128)(2,1)S(1)}, u32[]{:S(2)}, u32[]{:S(2)}) collective-permute-start(bf16[224,512]{1,0:T(8,128)(2,1)S(1)} %collective-permute-done.20.refs_1_), channel_id=1, source_target_pairs={{0,1},{1,0},{2,3},{3,2},{4,5},{5,4},{6,7},{7,6},{8,9},{9,8},{10,11... | collective-permute-start | bytes 688136 | tf_op jit(solution)/shard_map/ppermute | solution.py:714
  129.9 6.0 %copy-start.7 = (bf16[224,512]{1,0:T(8,128)(2,1)}, bf16[224,512]{1,0:T(8,128)(2,1)S(1)}, u32[]{:S(2)}) copy-start(bf16[224,512]{1,0:T(8,128)(2,1)S(1)} %collective-permute-done.18.refs_2_) | copy-start | bytes 688132
  129.9 11.0 %collective-permute-start.19 = (bf16[224,512]{1,0:T(8,128)(2,1)S(1)}, bf16[224,512]{1,0:T(8,128)(2,1)S(1)}, u32[]{:S(2)}, u32[]{:S(2)}) collective-permute-start(bf16[224,512]{1,0:T(8,128)(2,1)S(1)} %collective-permute-done.18.refs_2_), channel_id=1, source_target_pairs={{0,16},{16,0},{1,17},{17,1},{2,18},{18,2},{3,19},{19,3},{4,20},{20... | collective-permute-start | bytes 688136 | tf_op jit(solution)/shard_map/ppermute | solution.py:714
  132.8 3.1 %copy-start.9 = (bf16[224,512]{1,0:T(8,128)(2,1)}, bf16[224,512]{1,0:T(8,128)(2,1)S(1)}, u32[]{:S(2)}) copy-start(bf16[224,512]{1,0:T(8,128)(2,1)S(1)} %collective-permute-done.22.refs_3_) | copy-start | bytes 688132
  132.8 8.6 %collective-permute-start.23 = (bf16[224,512]{1,0:T(8,128)(2,1)S(1)}, bf16[224,512]{1,0:T(8,128)(2,1)}, u32[]{:S(2)}, u32[]{:S(2)}) collective-permute-start(bf16[224,512]{1,0:T(8,128)(2,1)S(1)} %collective-permute-done.22.refs_3_), channel_id=1, source_target_pairs={{0,8},{8,0},{1,9},{9,1},{2,10},{10,2},{3,11},{11,3},{4,12},{12,4},... | collective-permute-start | bytes 688136 | tf_op jit(solution)/shard_map/ppermute | solution.py:714
  135.3 6.1 %collective-permute-start.25 = (bf16[224,512]{1,0:T(8,128)(2,1)S(1)}, bf16[224,512]{1,0:T(8,128)(2,1)}, u32[]{:S(2)}, u32[]{:S(2)}) collective-permute-start(bf16[224,512]{1,0:T(8,128)(2,1)S(1)} %collective-permute-done.18.refs_2_), channel_id=1, source_target_pairs={{0,8},{8,0},{1,9},{9,1},{2,10},{10,2},{3,11},{11,3},{4,12},{12,4},... | collective-permute-start | bytes 688136 | tf_op jit(solution)/shard_map/ppermute | solution.py:714
  135.8 5.6 %collective-permute-start.27 = (bf16[224,512]{1,0:T(8,128)(2,1)S(1)}, bf16[224,512]{1,0:T(8,128)(2,1)}, u32[]{:S(2)}, u32[]{:S(2)}) collective-permute-start(bf16[224,512]{1,0:T(8,128)(2,1)S(1)} %collective-permute-done.26.refs_4_), channel_id=1, source_target_pairs={{0,8},{8,0},{1,9},{9,1},{2,10},{10,2},{3,11},{11,3},{4,12},{12,4},... | collective-permute-start | bytes 688136 | tf_op jit(solution)/shard_map/ppermute | solution.py:714
  140.7 1.8 %collective-permute-start.24 = (bf16[224,512]{1,0:T(8,128)(2,1)}, bf16[224,512]{1,0:T(8,128)(2,1)S(1)}, u32[]{:S(2)}, u32[]{:S(2)}) collective-permute-start(bf16[224,512]{1,0:T(8,128)(2,1)} %copy-done.6), channel_id=1, source_target_pairs={{0,8},{8,0},{1,9},{9,1},{2,10},{10,2},{3,11},{11,3},{4,12},{12,4},... | collective-permute-start | bytes 688136 | tf_op jit(solution)/shard_map/ppermute | solution.py:714
  140.9 1.7 %collective-permute-start.29 = (bf16[224,512]{1,0:T(8,128)(2,1)S(1)}, bf16[224,512]{1,0:T(8,128)(2,1)S(1)}, u32[]{:S(2)}, u32[]{:S(2)}) collective-permute-start(bf16[224,512]{1,0:T(8,128)(2,1)S(1)} %collective-permute-done.19.refs_0_), channel_id=1, source_target_pairs={{0,8},{8,0},{1,9},{9,1},{2,10},{10,2},{3,11},{11,3},{4,12},{12,4},... | collective-permute-start | bytes 688136 | tf_op jit(solution)/shard_map/ppermute | solution.py:714
  141.3 1.6 %collective-permute-start.30 = (bf16[224,512]{1,0:T(8,128)(2,1)S(1)}, bf16[224,512]{1,0:T(8,128)(2,1)S(1)}, u32[]{:S(2)}, u32[]{:S(2)}) collective-permute-start(bf16[224,512]{1,0:T(8,128)(2,1)S(1)} %collective-permute-done.21.refs_1_), channel_id=1, source_target_pairs={{0,8},{8,0},{1,9},{9,1},{2,10},{10,2},{3,11},{11,3},{4,12},{12,4},... | collective-permute-start | bytes 688136 | tf_op jit(solution)/shard_map/ppermute | solution.py:714
  (19 other events, 23.7 us)

commit v2 on v1

--- a/solution.py
+++ b/solution.py
@@ -835,12 +835,15 @@
         partial(line_kernel, len(sides)),
         "line",
         (packed(part + SMALL, width),) * depth,
-        *after((parts[0], *got), returned, returned_rims),
+        *after((parts[0], *got), returned, returned_rims[:2]),
         scratch=[pltpu.VMEM((part * depth + SMALL, width), BF16)],
     )
     got = [ahead(parts[step], step) for step in range(1, depth)]
     own, small = call(
-        total_kernel, "total", (packed(part, width), wide(SMALL, width)), parts[0], *got
+        total_kernel,
+        "total",
+        (packed(part, width), wide(SMALL, width)),
+        *after((parts[0], *got), returned_rims[2:]),
     )
     lines, bit = {0: own}, depth // 2
     while bit:

time: 148 us -> 148 us (level)
  starting transfers between devices: 52.2 us -> 43.3 us
  waiting for transfers between devices: 38.9 us -> 47.5 us
    all_to_all x2, waiting for transfers between devices: 0.01 us -> 16.5 us  [exchanged(): lax.all_to_all(parts, everyone, split_axis=0, concat_axis=0, tiled=True)]
    ppermute x3, waiting for transfers between devices: 6.5 us -> 0.01 us  [ahead(): lax.ppermute(array, 'z', [(i, (i + step) % size) for i in range(size)])]
    ppermute x3, starting transfers between devices: 10 us -> 4.64 us  [shards(): lax.ppermute(piece, 'z', [(i, i ^ bit) for i in range(depth)])]
    ppermute x8, waiting for transfers between devices: 15.4 us -> 10.8 us  [swap(): return lax.ppermute(array, axes, pairs)]
    ppermute x8, starting transfers between devices: 12.3 us -> 9.19 us  [swap(): return lax.ppermute(array, axes, pairs)]
    ppermute x17, waiting for transfers between devices: 11.6 us -> 13.2 us  [across(): return lax.ppermute(array, axes, [(i, last - i) for i in range(last + 1)])]
    ppermute x3, waiting for transfers between devices: 5.4 us -> 6.94 us  [shards(): lax.ppermute(piece, 'z', [(i, i ^ bit) for i in range(depth)])]
  transfers between devices with their start and end apart: 33 -> 33, of which waited for: 13 -> 14; matrix products, arithmetic and copies ran while one was open for 0% -> 0% of each run, Pallas kernels for 5% -> 5%
where the time goes in v2:
time: 148 us; the launch traced here: 147 us
  Pallas kernels  48.9 us (33%)
  waiting for transfers between devices  47.5 us (32%)
  starting transfers between devices  43.3 us (29%)
  local copies, waits for them, and re-layouts  5.73 us (4%)
  between operations  1.74 us (1%)
    pallas_call x1, Pallas kernels, shards(): pl.pallas_call(partial(passes_kernel, peers, capacity, node_rows + rims,...  26.3 us
    all_to_all x2, waiting for transfers between devices, exchanged(): lax.all_to_all(parts, everyone, split_axis=0, concat_axis=0, tiled=True)  16.5 us
    pallas_call x6, Pallas kernels, call(): pl.pallas_call(kernel, out_shape=out_shape, scratch_shapes=scratch, compi...  14.8 us
    ppermute x17, waiting for transfers between devices, across(): return lax.ppermute(array, axes, [(i, last - i) for i in range(last + 1)])  13.2 us
    ppermute x17, starting transfers between devices, across(): return lax.ppermute(array, axes, [(i, last - i) for i in range(last + 1)])  13.2 us
    all_to_all x2, starting transfers between devices, exchanged(): lax.all_to_all(parts, everyone, split_axis=0, concat_axis=0, tiled=True)  12.4 us
    ppermute x8, waiting for transfers between devices, swap(): return lax.ppermute(array, axes, pairs)  10.8 us
    ppermute x8, starting transfers between devices, swap(): return lax.ppermute(array, axes, pairs)  9.19 us
  transfers between devices with their start and end apart: 33, of which 14 were waited for; matrix products, arithmetic and copies ran while one was open for 0% of the time, Pallas kernels for 5%

profile of v2, /device:TPU:0, one launch (start us, length us, event | category | flops | bytes accessed | tf_op | source)
XLA Modules:
  0.0 147.1 jit_solution(12547500477551365236)
XLA Ops:
  0.6 2.1 %pick.1 = (f32[256,128]{1,0:T(8,128)}, bf16[32,512]{1,0:T(8,128)(2,1)}, bf16[32,512]{1,0:T(8,128)(2,1)}, bf16[32,512]{1,0:T(8,128)(2,1)}, bf16[32,512]{1,0:T(8,128)(2,1)}) custom-call(s32[1,4,32]{2,1,0:T(4,128)} %halo_ref.2, s32[1,2,32]{2,1,0:T(2,128)} %bitcast.14, bf16[256,512]{1,0:T(8,128)(2,1)} %refs_5_.1), custom_call_target="tpu_custom_call" | custom-call | tf_op jit(solution)/shard_map/pick/pallas_call | solution.py:698
  2.7 7.3 %all-to-all-start = ((f32[32,8,128]{2,1,0:T(8,128)}), f32[32,8,128]{2,1,0:T(8,128)S(1)}, u32[]{:S(2)}, u32[]{:S(2)}) async-start(f32[32,8,128]{2,1,0:T(8,128)} %bitcast.13), calls=%async_computation | async-start | bytes 262144 | tf_op jit(solution)/shard_map/all_to_all | solution.py:693
  10.3 0.7 collective-permute-start.1
  11.0 1.7 %collective-permute-start.2 = (bf16[32,512]{1,0:T(8,128)(2,1)}, bf16[32,512]{1,0:T(8,128)(2,1)S(1)}, u32[]{:S(2)}, u32[]{:S(2)}) collective-permute-start(bf16[32,512]{1,0:T(8,128)(2,1)} %get-tuple-element.79), channel_id=1, source_target_pairs={{0,1},{1,0},{2,3},{3,2},{4,5},{5,4},{6,7},{7,6},{8,9},{9,8},{10,11... | collective-permute-start | bytes 98312 | tf_op jit(solution)/shard_map/ppermute | solution.py:638
  12.7 3.3 %collective-permute-start.3 = (bf16[32,512]{1,0:T(8,128)(2,1)}, bf16[32,512]{1,0:T(8,128)(2,1)S(1)}, u32[]{:S(2)}, u32[]{:S(2)}) collective-permute-start(bf16[32,512]{1,0:T(8,128)(2,1)} %get-tuple-element.80), channel_id=1, source_target_pairs={{1,2},{2,1},{3,4},{4,3},{5,6},{6,5},{7,0},{0,7},{9,10},{10,9},{11,... | collective-permute-start | bytes 98312 | tf_op jit(solution)/shard_map/ppermute | solution.py:638
  16.8 2.8 %collective-permute-done.3.refs_9_ = bf16[32,512]{1,0:T(8,128)(2,1)S(1)} collective-permute-done((bf16[32,512]{1,0:T(8,128)(2,1)}, bf16[32,512]{1,0:T(8,128)(2,1)S(1)}, u32[]{:S(2)}, u32[]{:S(2)}) %collective-permute-start.3) | collective-permute-done | bytes 32800 | tf_op jit(solution)/shard_map/ppermute | solution.py:638
  19.6 0.6 copy-done.33
  20.2 26.3 %passes.1 = (bf16[2048,512]{1,0:T(8,128)(2,1)}, bf16[2048,512]{1,0:T(8,128)(2,1)}, bf16[256,512]{1,0:T(8,128)(2,1)}, f32[256,512]{1,0:T(8,128)}, f32[256,128]{1,...) custom-call(s32[1]{0:T(128)S(6)} %copy.37.refs_0_, ...), custom_call_target="tpu_custom_call" | custom-call | flops 20000000000 | bytes 20000000 | tf_op jit(solution)/shard_map/passes/pallas_call | solution.py:756
  46.5 1.5 %collective-permute-start.4 = (bf16[1824,512]{1,0:T(8,128)(2,1)}, bf16[1824,512]{1,0:T(8,128)(2,1)S(1)}, u32[]{:S(2)}, u32[]{:S(2)}) collective-permute-start(bf16[1824,512]{1,0:T(8,128)(2,1)} %get-tuple-element.91), channel_id=1, source_target_pairs={{0,8},{8,0},{1,9},{9,1},{2,10},{10,2},{3,11},{11,3},{4,12},{12,4},... | collective-permute-start | bytes 5603336 | tf_op jit(solution)/shard_map/ppermute | solution.py:714
  48.0 3.7 %collective-permute-done.4.got = bf16[1824,512]{1,0:T(8,128)(2,1)S(1)} collective-permute-done((bf16[1824,512]{1,0:T(8,128)(2,1)}, bf16[1824,512]{1,0:T(8,128)(2,1)S(1)}, u32[]{:S(2)}, u32[]{:S(2)}) %collective-permute-start.4) | collective-permute-done | bytes 1867808 | tf_op jit(solution)/shard_map/ppermute | solution.py:714
  51.7 1.2 copy-done
  53.0 3.7 %plane.1 = (bf16[464,512]{1,0:T(8,128)(2,1)}, bf16[464,512]{1,0:T(8,128)(2,1)}, bf16[464,512]{1,0:T(8,128)(2,1)}, bf16[464,512]{1,0:T(8,128)(2,1)}) custom-call(bf16[1824,512]{1,0:T(8,128)(2,1)} %get-tuple-element.90.keep, bf16[1824,512]{1,0:T(8,128)(2,1)} %copy-done), custom_call_target="tpu_custom_call" | custom-call | tf_op jit(solution)/shard_map/plane/pallas_call | solution.py:698
  56.6 2.2 %collective-permute-start.9 = (bf16[464,512]{1,0:T(8,128)(2,1)}, bf16[464,512]{1,0:T(8,128)(2,1)S(1)}, u32[]{:S(2)}, u32[]{:S(2)}) collective-permute-start(bf16[464,512]{1,0:T(8,128)(2,1)} %get-tuple-element.93), channel_id=1, source_target_pairs={{0,16},{16,0},{1,17},{17,1},{2,18},{18,2},{3,19},{19,3},{4,20},{20... | collective-permute-start | bytes 1425416 | tf_op jit(solution)/shard_map/ppermute | solution.py:714
  58.8 1.5 collective-permute-start.11
  60.3 5.1 %all-to-all-start.1 = ((f32[32,8,128]{2,1,0:T(8,128)}), f32[32,8,128]{2,1,0:T(8,128)S(1)}, u32[]{:S(2)}, u32[]{:S(2)}) async-start(f32[32,8,128]{2,1,0:T(8,128)} %bitcast.9), calls=%async_computation.1 | async-start | bytes 262144 | tf_op jit(solution)/shard_map/all_to_all | solution.py:693
  65.8 0.8 collective-permute-start.6
  66.7 16.5 %all-to-all-done.1 = f32[32,8,128]{2,1,0:T(8,128)S(1)} async-done(((f32[32,8,128]{2,1,0:T(8,128)}), f32[32,8,128]{2,1,0:T(8,128)S(1)}, u32[]{:S(2)}, u32[]{:S(2)}) %all-to-all-start.1) | async-done | bytes 131104 | tf_op jit(solution)/shard_map/all_to_all | solution.py:693
  83.3 0.8 copy-done.2
  84.4 2.7 %line.1 = (bf16[128,512]{1,0:T(8,128)(2,1)}, bf16[128,512]{1,0:T(8,128)(2,1)}, bf16[128,512]{1,0:T(8,128)(2,1)}, bf16[128,512]{1,0:T(8,128)(2,1)}) custom-call(bf16[464,512]{1,0:T(8,128)(2,1)} %get-tuple-element.101.refs_0_, bf16[464,512]{1,0:T(8,128)(2,1)} %copy-done.2, bf16[464,512]{1,0:T(8,128)(2,1)} %copy-done.3, bf16[464,512]{1,0:T(8,128)(2,1)} %copy-done.4), custom_call_target="tpu_custom_call" | custom-call | tf_op jit(solution)/shard_map/line/pallas_call | solution.py:698
  87.1 2.7 %collective-permute-start.13 = (bf16[128,512]{1,0:T(8,128)(2,1)}, bf16[128,512]{1,0:T(8,128)(2,1)S(1)}, u32[]{:S(2)}, u32[]{:S(2)}) collective-permute-start(bf16[128,512]{1,0:T(8,128)(2,1)} %get-tuple-element.107), channel_id=1, source_target_pairs={{0,4},{2,6},{4,0},{6,2},{1,5},{3,7},{5,1},{7,3},{8,12},{10,14},{12... | collective-permute-start | bytes 393224 | tf_op jit(solution)/shard_map/ppermute | solution.py:718
  89.8 1.1 collective-permute-start.14
  90.9 0.6 collective-permute-start.7
  91.5 1.5 collective-permute-start.8
  92.9 1.9 %collective-permute-done.7.refs_2_ = bf16[32,512]{1,0:T(8,128)(2,1)S(1)} collective-permute-done((bf16[32,512]{1,0:T(8,128)(2,1)S(1)}, bf16[32,512]{1,0:T(8,128)(2,1)S(1)}, u32[]{:S(2)}, u32[]{:S(2)}) %collective-permute-start.7) | collective-permute-done | bytes 32800 | tf_op jit(solution)/shard_map/ppermute | solution.py:638
  94.8 6.0 %collective-permute-done.8.refs_3_ = bf16[32,512]{1,0:T(8,128)(2,1)S(1)} collective-permute-done((bf16[32,512]{1,0:T(8,128)(2,1)S(1)}, bf16[32,512]{1,0:T(8,128)(2,1)S(1)}, u32[]{:S(2)}, u32[]{:S(2)}) %collective-permute-start.8) | collective-permute-done | bytes 32800 | tf_op jit(solution)/shard_map/ppermute | solution.py:638
  100.8 0.6 copy-done.16
  101.5 1.8 %total.1 = (bf16[112,512]{1,0:T(8,128)(2,1)}, f32[16,512]{1,0:T(8,128)}) custom-call(bf16[128,512]{1,0:T(8,128)(2,1)} %get-tuple-element.109.refs_0_, bf16[128,512]{1,0:T(8,128)(2,1)} %copy-done.16, bf16[128,512]{1,0:T(8,128)(2,1)} %copy-done.17, bf16[128,512]{1,0:T(8,128)(2,1)} %copy-done.18), custom_call_target="tpu_custom_call" | custom-call | tf_op jit(solution)/shard_map/total/pallas_call | solution.py:698
  103.4 1.7 %collective-permute-start.16 = (bf16[112,512]{1,0:T(8,128)(2,1)}, bf16[112,512]{1,0:T(8,128)(2,1)S(1)}, u32[]{:S(2)}, u32[]{:S(2)}) collective-permute-start(bf16[112,512]{1,0:T(8,128)(2,1)} %get-tuple-element.113.refs_0_), channel_id=1, source_target_pairs={{0,4},{2,6},{4,0},{6,2},{1,5},{3,7},{5,1},{7,3},{8,12},{10,14},{12... | collective-permute-start | bytes 344072 | tf_op jit(solution)/shard_map/ppermute | solution.py:851
  105.1 1.4 collective-permute-start.15
  106.5 3.7 %collective-permute-done.16.refs_2_ = bf16[112,512]{1,0:T(8,128)(2,1)S(1)} collective-permute-done((bf16[112,512]{1,0:T(8,128)(2,1)}, bf16[112,512]{1,0:T(8,128)(2,1)S(1)}, u32[]{:S(2)}, u32[]{:S(2)}) %collective-permute-start.16) | collective-permute-done | bytes 114720 | tf_op jit(solution)/shard_map/ppermute | solution.py:851
  110.2 1.5 %collective-permute-start.17 = (bf16[112,512]{1,0:T(8,128)(2,1)S(1)}, bf16[112,512]{1,0:T(8,128)(2,1)S(1)}, u32[]{:S(2)}, u32[]{:S(2)}) collective-permute-start(bf16[112,512]{1,0:T(8,128)(2,1)S(1)} %collective-permute-done.16.refs_2_), channel_id=1, source_target_pairs={{0,2},{2,0},{4,6},{6,4},{1,3},{3,1},{5,7},{7,5},{8,10},{10,8},{12,... | collective-permute-start | bytes 344072 | tf_op jit(solution)/shard_map/ppermute | solution.py:851
  111.7 3.2 %collective-permute-done.17.refs_3_ = bf16[112,512]{1,0:T(8,128)(2,1)S(1)} collective-permute-done((bf16[112,512]{1,0:T(8,128)(2,1)S(1)}, bf16[112,512]{1,0:T(8,128)(2,1)S(1)}, u32[]{:S(2)}, u32[]{:S(2)}) %collective-permute-start.17) | collective-permute-done | bytes 114720 | tf_op jit(solution)/shard_map/ppermute | solution.py:851
  115.0 0.6 copy-done.21
  115.6 2.0 %join.1 = (bf16[448,512]{1,0:T(8,128)(2,1)}, bf16[224,512]{1,0:T(8,128)(2,1)}, bf16[224,512]{1,0:T(8,128)(2,1)}) custom-call(bf16[112,512]{1,0:T(8,128)(2,1)} %get-tuple-element.113.refs_0_, bf16[112,512]{1,0:T(8,128)(2,1)} %copy-done.20, bf16[112,512]{1,0:T(8,128)(2,1)} %copy-done.19, bf16[112,512]{1,0:T(8,128)(2,1)} %copy-done.21), custom_call_target="tpu_custom_call" | custom-call | tf_op jit(solution)/shard_map/join/pallas_call | solution.py:698
  117.6 3.2 %collective-permute-start.20 = (bf16[224,512]{1,0:T(8,128)(2,1)}, bf16[224,512]{1,0:T(8,128)(2,1)S(1)}, u32[]{:S(2)}, u32[]{:S(2)}) collective-permute-start(bf16[224,512]{1,0:T(8,128)(2,1)} %get-tuple-element.125), channel_id=1, source_target_pairs={{0,16},{16,0},{1,17},{17,1},{2,18},{18,2},{3,19},{19,3},{4,20},{20... | collective-permute-start | bytes 688136 | tf_op jit(solution)/shard_map/ppermute | solution.py:714
  121.3 0.7 collective-permute-start.22
  122.0 1.0 collective-permute-start.26
  123.0 4.6 %collective-permute-done.20.refs_1_ = bf16[224,512]{1,0:T(8,128)(2,1)S(1)} collective-permute-done((bf16[224,512]{1,0:T(8,128)(2,1)}, bf16[224,512]{1,0:T(8,128)(2,1)S(1)}, u32[]{:S(2)}, u32[]{:S(2)}) %collective-permute-start.20) | collective-permute-done | bytes 229408 | tf_op jit(solution)/shard_map/ppermute | solution.py:714
  127.5 1.0 collective-permute-start.21
  128.5 1.0 collective-permute-done.18.refs_2_
  129.5 0.4 collective-permute-start.19
  130.0 2.5 %collective-permute-done.22.refs_3_ = bf16[224,512]{1,0:T(8,128)(2,1)S(1)} collective-permute-done((bf16[224,512]{1,0:T(8,128)(2,1)}, bf16[224,512]{1,0:T(8,128)(2,1)S(1)}, u32[]{:S(2)}, u32[]{:S(2)}) %collective-permute-start.22) | collective-permute-done | bytes 229408 | tf_op jit(solution)/shard_map/ppermute | solution.py:714
  132.5 2.5 %returned.1 = bf16[256,512]{1,0:T(8,128)(2,1)} custom-call(s32[1,4,32]{2,1,0:T(4,128)} %halo_ref.2, s32[1,2,32]{2,1,0:T(2,128)} %bitcast.15, f32[256,512]{1,0:T(8,128)} %get-tuple-element.117.totals_ref, f32[256,128]{1,0:T(8,128)} %bitcast.11, bf16[32,512]{1,0:T(8,128)(2,1)} %copy-done.22, bf16[32,512]{1,0:T(8,128)(2,1)} %copy-done.23, ...), custom_call_target="tpu_custom_call" | custom-call | tf_op jit(solution)/shard_map/returned/pallas_call | solution.py:698
  135.0 0.5 collective-permute-start.25
  135.7 0.6 copy-done.5
  136.2 4.2 %finish.2 = (f32[1536,512]{1,0:T(8,128)}, f32[512,512]{1,0:T(8,128)}, f32[1024,512]{1,0:T(8,128)}, f32[512,512]{1,0:T(8,128)}, f32[512]{0:T(512)}, /*index=5*/f32[512]{0:T(512)}, f32[512]{0:T(512)}, f32[512]{0:T(512)}) custom-call(bf16[448,512]{1,0:T(8,128)(2,1)} %get-tuple-element.114.refs_0_, bf16[224,512]{1,0:T(8,128)(2,1)} %copy-done.6, ...), custom_call_target="tpu_custom_call" | custom-call | tf_op jit(solution)/shard_map/finish/pallas_call | solution.py:875
  141.1 1.1 collective-permute-done.24.refs_3_
  143.3 3.7 %finish.3 = (f32[1536,512]{1,0:T(8,128)}, f32[512,512]{1,0:T(8,128)}, f32[1024,512]{1,0:T(8,128)}, f32[512,512]{1,0:T(8,128)}) custom-call(bf16[224,512]{1,0:T(8,128)(2,1)} %copy-done.11, bf16[224,512]{1,0:T(8,128)(2,1)} %copy-done.10, ...), custom_call_target="tpu_custom_call", output_to_operand_aliasing={{0}: (8, {}), {1}: (9, {}), {2}: (10, {}), {3}: (11, {})} | custom-call | tf_op jit(solution)/shard_map/finish/pallas_call | solution.py:875
  (95 shorter events, 3.8 us)
Async XLA Ops:
  2.7 16.8 %all-to-all-start = ((f32[32,8,128]{2,1,0:T(8,128)}), f32[32,8,128]{2,1,0:T(8,128)S(1)}, u32[]{:S(2)}, u32[]{:S(2)}) async-start(f32[32,8,128]{2,1,0:T(8,128)} %bitcast.13), calls=%async_computation | async-start | bytes 262144 | tf_op jit(solution)/shard_map/all_to_all | solution.py:693
  10.0 6.7 %collective-permute-start = (bf16[32,512]{1,0:T(8,128)(2,1)}, bf16[32,512]{1,0:T(8,128)(2,1)S(1)}, u32[]{:S(2)}, u32[]{:S(2)}) collective-permute-start(bf16[32,512]{1,0:T(8,128)(2,1)} %get-tuple-element.77), channel_id=1, source_target_pairs={{0,8},{8,0},{16,24},{24,16},{1,9},{9,1},{17,25},{25,17},{2,10},{10... | collective-permute-start | bytes 98312 | tf_op jit(solution)/shard_map/ppermute | solution.py:638
  10.3 6.4 %collective-permute-start.1 = (bf16[32,512]{1,0:T(8,128)(2,1)}, bf16[32,512]{1,0:T(8,128)(2,1)S(1)}, u32[]{:S(2)}, u32[]{:S(2)}) collective-permute-start(bf16[32,512]{1,0:T(8,128)(2,1)} %get-tuple-element.78), channel_id=1, source_target_pairs={{8,16},{16,8},{9,17},{17,9},{10,18},{18,10},{11,19},{19,11},{12,20... | collective-permute-start | bytes 98312 | tf_op jit(solution)/shard_map/ppermute | solution.py:638
  11.0 5.7 %collective-permute-start.2 = (bf16[32,512]{1,0:T(8,128)(2,1)}, bf16[32,512]{1,0:T(8,128)(2,1)S(1)}, u32[]{:S(2)}, u32[]{:S(2)}) collective-permute-start(bf16[32,512]{1,0:T(8,128)(2,1)} %get-tuple-element.79), channel_id=1, source_target_pairs={{0,1},{1,0},{2,3},{3,2},{4,5},{5,4},{6,7},{7,6},{8,9},{9,8},{10,11... | collective-permute-start | bytes 98312 | tf_op jit(solution)/shard_map/ppermute | solution.py:638
  12.7 6.8 %collective-permute-start.3 = (bf16[32,512]{1,0:T(8,128)(2,1)}, bf16[32,512]{1,0:T(8,128)(2,1)S(1)}, u32[]{:S(2)}, u32[]{:S(2)}) collective-permute-start(bf16[32,512]{1,0:T(8,128)(2,1)} %get-tuple-element.80), channel_id=1, source_target_pairs={{1,2},{2,1},{3,4},{4,3},{5,6},{6,5},{7,0},{0,7},{9,10},{10,9},{11,... | collective-permute-start | bytes 98312 | tf_op jit(solution)/shard_map/ppermute | solution.py:638
  16.7 2.9 %copy-start.30 = (bf16[32,512]{1,0:T(8,128)(2,1)}, bf16[32,512]{1,0:T(8,128)(2,1)S(1)}, u32[]{:S(2)}) copy-start(bf16[32,512]{1,0:T(8,128)(2,1)S(1)} %collective-permute-done.refs_6_) | copy-start | bytes 98308
  46.5 18.9 %copy-start.29 = (bf16[32,512]{1,0:T(8,128)(2,1)S(1)}, bf16[32,512]{1,0:T(8,128)(2,1)}, u32[]{:S(2)}) copy-start(bf16[32,512]{1,0:T(8,128)(2,1)} %get-tuple-element.97) | copy-start | bytes 98308
  46.5 19.2 %copy-start.28 = (bf16[32,512]{1,0:T(8,128)(2,1)S(1)}, bf16[32,512]{1,0:T(8,128)(2,1)}, u32[]{:S(2)}) copy-start(bf16[32,512]{1,0:T(8,128)(2,1)} %get-tuple-element.98) | copy-start | bytes 98308
  46.5 5.2 %collective-permute-start.4 = (bf16[1824,512]{1,0:T(8,128)(2,1)}, bf16[1824,512]{1,0:T(8,128)(2,1)S(1)}, u32[]{:S(2)}, u32[]{:S(2)}) collective-permute-start(bf16[1824,512]{1,0:T(8,128)(2,1)} %get-tuple-element.91), channel_id=1, source_target_pairs={{0,8},{8,0},{1,9},{9,1},{2,10},{10,2},{3,11},{11,3},{4,12},{12,4},... | collective-permute-start | bytes 5603336 | tf_op jit(solution)/shard_map/ppermute | solution.py:714
  53.0 37.9 %copy-start.27 = (bf16[32,512]{1,0:T(8,128)(2,1)S(1)}, bf16[32,512]{1,0:T(8,128)(2,1)}, u32[]{:S(2)}) copy-start(bf16[32,512]{1,0:T(8,128)(2,1)} %get-tuple-element.99) | copy-start | bytes 98308
  53.0 38.5 %copy-start.26 = (bf16[32,512]{1,0:T(8,128)(2,1)S(1)}, bf16[32,512]{1,0:T(8,128)(2,1)}, u32[]{:S(2)}) copy-start(bf16[32,512]{1,0:T(8,128)(2,1)} %get-tuple-element.100) | copy-start | bytes 98308
  56.6 26.6 %collective-permute-start.9 = (bf16[464,512]{1,0:T(8,128)(2,1)}, bf16[464,512]{1,0:T(8,128)(2,1)S(1)}, u32[]{:S(2)}, u32[]{:S(2)}) collective-permute-start(bf16[464,512]{1,0:T(8,128)(2,1)} %get-tuple-element.93), channel_id=1, source_target_pairs={{0,16},{16,0},{1,17},{17,1},{2,18},{18,2},{3,19},{19,3},{4,20},{20... | collective-permute-start | bytes 1425416 | tf_op jit(solution)/shard_map/ppermute | solution.py:714
  58.8 24.4 %collective-permute-start.10 = (bf16[464,512]{1,0:T(8,128)(2,1)}, bf16[464,512]{1,0:T(8,128)(2,1)S(1)}, u32[]{:S(2)}, u32[]{:S(2)}) collective-permute-start(bf16[464,512]{1,0:T(8,128)(2,1)} %get-tuple-element.94), channel_id=1, source_target_pairs={{0,1},{1,0},{2,3},{3,2},{4,5},{5,4},{6,7},{7,6},{8,9},{9,8},{10,11... | collective-permute-start | bytes 1425416 | tf_op jit(solution)/shard_map/ppermute | solution.py:714
  58.8 24.5 %collective-permute-start.11 = (bf16[464,512]{1,0:T(8,128)(2,1)}, bf16[464,512]{1,0:T(8,128)(2,1)S(1)}, u32[]{:S(2)}, u32[]{:S(2)}) collective-permute-start(bf16[464,512]{1,0:T(8,128)(2,1)} %get-tuple-element.95), channel_id=1, source_target_pairs={{0,17},{1,16},{16,1},{17,0},{2,19},{3,18},{18,3},{19,2},{4,21},{5,... | collective-permute-start | bytes 1425416 | tf_op jit(solution)/shard_map/ppermute | solution.py:714
  60.3 23.0 %all-to-all-start.1 = ((f32[32,8,128]{2,1,0:T(8,128)}), f32[32,8,128]{2,1,0:T(8,128)S(1)}, u32[]{:S(2)}, u32[]{:S(2)}) async-start(f32[32,8,128]{2,1,0:T(8,128)} %bitcast.9), calls=%async_computation.1 | async-start | bytes 262144 | tf_op jit(solution)/shard_map/all_to_all | solution.py:693
  65.4 1.3 collective-permute-start.5
  65.8 1.0 collective-permute-start.6
  66.7 65.7 %copy-start.22 = (bf16[32,512]{1,0:T(8,128)(2,1)}, bf16[32,512]{1,0:T(8,128)(2,1)S(1)}, u32[]{:S(2)}) copy-start(bf16[32,512]{1,0:T(8,128)(2,1)S(1)} %collective-permute-done.5.refs_0_) | copy-start | bytes 98308
  66.7 65.7 %copy-start.23 = (bf16[32,512]{1,0:T(8,128)(2,1)}, bf16[32,512]{1,0:T(8,128)(2,1)S(1)}, u32[]{:S(2)}) copy-start(bf16[32,512]{1,0:T(8,128)(2,1)S(1)} %collective-permute-done.6.refs_1_) | copy-start | bytes 98308
  83.3 49.2 %copy-start.1 = (f32[32,8,128]{2,1,0:T(8,128)}, f32[32,8,128]{2,1,0:T(8,128)S(1)}, u32[]{:S(2)}) copy-start(f32[32,8,128]{2,1,0:T(8,128)S(1)} %all-to-all-done.1) | copy-start | bytes 393220
  87.1 13.7 %collective-permute-start.12 = (bf16[128,512]{1,0:T(8,128)(2,1)}, bf16[128,512]{1,0:T(8,128)(2,1)S(1)}, u32[]{:S(2)}, u32[]{:S(2)}) collective-permute-start(bf16[128,512]{1,0:T(8,128)(2,1)} %get-tuple-element.106), channel_id=1, source_target_pairs={{0,2},{2,4},{4,6},{6,0},{1,3},{3,5},{5,7},{7,1},{8,10},{10,12},{12... | collective-permute-start | bytes 393224 | tf_op jit(solution)/shard_map/ppermute | solution.py:718
  87.1 13.7 %collective-permute-start.13 = (bf16[128,512]{1,0:T(8,128)(2,1)}, bf16[128,512]{1,0:T(8,128)(2,1)S(1)}, u32[]{:S(2)}, u32[]{:S(2)}) collective-permute-start(bf16[128,512]{1,0:T(8,128)(2,1)} %get-tuple-element.107), channel_id=1, source_target_pairs={{0,4},{2,6},{4,0},{6,2},{1,5},{3,7},{5,1},{7,3},{8,12},{10,14},{12... | collective-permute-start | bytes 393224 | tf_op jit(solution)/shard_map/ppermute | solution.py:718
  89.8 11.1 %collective-permute-start.14 = (bf16[128,512]{1,0:T(8,128)(2,1)}, bf16[128,512]{1,0:T(8,128)(2,1)S(1)}, u32[]{:S(2)}, u32[]{:S(2)}) collective-permute-start(bf16[128,512]{1,0:T(8,128)(2,1)} %get-tuple-element.108), channel_id=1, source_target_pairs={{0,6},{2,0},{4,2},{6,4},{1,7},{3,1},{5,3},{7,5},{8,14},{10,8},{12,... | collective-permute-start | bytes 393224 | tf_op jit(solution)/shard_map/ppermute | solution.py:718
  90.9 3.9 %collective-permute-start.7 = (bf16[32,512]{1,0:T(8,128)(2,1)S(1)}, bf16[32,512]{1,0:T(8,128)(2,1)S(1)}, u32[]{:S(2)}, u32[]{:S(2)}) collective-permute-start(bf16[32,512]{1,0:T(8,128)(2,1)S(1)} %copy-done.27), channel_id=1, source_target_pairs={{0,1},{1,0},{2,3},{3,2},{4,5},{5,4},{6,7},{7,6},{8,9},{9,8},{10,11... | collective-permute-start | bytes 98312 | tf_op jit(solution)/shard_map/ppermute | solution.py:638
  91.5 9.3 %collective-permute-start.8 = (bf16[32,512]{1,0:T(8,128)(2,1)S(1)}, bf16[32,512]{1,0:T(8,128)(2,1)S(1)}, u32[]{:S(2)}, u32[]{:S(2)}) collective-permute-start(bf16[32,512]{1,0:T(8,128)(2,1)S(1)} %copy-done.26), channel_id=1, source_target_pairs={{1,2},{2,1},{3,4},{4,3},{5,6},{6,5},{7,0},{0,7},{9,10},{10,9},{11,... | collective-permute-start | bytes 98312 | tf_op jit(solution)/shard_map/ppermute | solution.py:638
  94.8 33.7 %copy-start.24 = (bf16[32,512]{1,0:T(8,128)(2,1)}, bf16[32,512]{1,0:T(8,128)(2,1)S(1)}, u32[]{:S(2)}) copy-start(bf16[32,512]{1,0:T(8,128)(2,1)S(1)} %collective-permute-done.7.refs_2_) | copy-start | bytes 98308
  100.8 27.8 %copy-start.25 = (bf16[32,512]{1,0:T(8,128)(2,1)}, bf16[32,512]{1,0:T(8,128)(2,1)S(1)}, u32[]{:S(2)}) copy-start(bf16[32,512]{1,0:T(8,128)(2,1)S(1)} %collective-permute-done.8.refs_3_) | copy-start | bytes 98308
  103.4 6.8 %collective-permute-start.16 = (bf16[112,512]{1,0:T(8,128)(2,1)}, bf16[112,512]{1,0:T(8,128)(2,1)S(1)}, u32[]{:S(2)}, u32[]{:S(2)}) collective-permute-start(bf16[112,512]{1,0:T(8,128)(2,1)} %get-tuple-element.113.refs_0_), channel_id=1, source_target_pairs={{0,4},{2,6},{4,0},{6,2},{1,5},{3,7},{5,1},{7,3},{8,12},{10,14},{12... | collective-permute-start | bytes 344072 | tf_op jit(solution)/shard_map/ppermute | solution.py:851
  105.1 6.6 %collective-permute-start.15 = (bf16[112,512]{1,0:T(8,128)(2,1)}, bf16[112,512]{1,0:T(8,128)(2,1)S(1)}, u32[]{:S(2)}, u32[]{:S(2)}) collective-permute-start(bf16[112,512]{1,0:T(8,128)(2,1)} %get-tuple-element.113.refs_0_), channel_id=1, source_target_pairs={{0,2},{2,0},{4,6},{6,4},{1,3},{3,1},{5,7},{7,5},{8,10},{10,8},{12,... | collective-permute-start | bytes 344072 | tf_op jit(solution)/shard_map/ppermute | solution.py:851
  110.2 4.8 %copy-start.19 = (bf16[112,512]{1,0:T(8,128)(2,1)}, bf16[112,512]{1,0:T(8,128)(2,1)S(1)}, u32[]{:S(2)}) copy-start(bf16[112,512]{1,0:T(8,128)(2,1)S(1)} %collective-permute-done.16.refs_2_) | copy-start | bytes 344068
  110.2 4.8 %collective-permute-start.17 = (bf16[112,512]{1,0:T(8,128)(2,1)S(1)}, bf16[112,512]{1,0:T(8,128)(2,1)S(1)}, u32[]{:S(2)}, u32[]{:S(2)}) collective-permute-start(bf16[112,512]{1,0:T(8,128)(2,1)S(1)} %collective-permute-done.16.refs_2_), channel_id=1, source_target_pairs={{0,2},{2,0},{4,6},{6,4},{1,3},{3,1},{5,7},{7,5},{8,10},{10,8},{12,... | collective-permute-start | bytes 344072 | tf_op jit(solution)/shard_map/ppermute | solution.py:851
  111.7 3.2 %copy-start.20 = (bf16[112,512]{1,0:T(8,128)(2,1)}, bf16[112,512]{1,0:T(8,128)(2,1)S(1)}, u32[]{:S(2)}) copy-start(bf16[112,512]{1,0:T(8,128)(2,1)S(1)} %collective-permute-done.15.refs_1_) | copy-start | bytes 344068
  117.6 17.8 %collective-permute-start.28 = (bf16[448,512]{1,0:T(8,128)(2,1)}, bf16[448,512]{1,0:T(8,128)(2,1)S(1)}, u32[]{:S(2)}, u32[]{:S(2)}) collective-permute-start(bf16[448,512]{1,0:T(8,128)(2,1)} %get-tuple-element.114.refs_0_), channel_id=1, source_target_pairs={{0,8},{8,0},{1,9},{9,1},{2,10},{10,2},{3,11},{11,3},{4,12},{12,4},... | collective-permute-start | bytes 1376264 | tf_op jit(solution)/shard_map/ppermute | solution.py:714
  117.6 9.9 %collective-permute-start.20 = (bf16[224,512]{1,0:T(8,128)(2,1)}, bf16[224,512]{1,0:T(8,128)(2,1)S(1)}, u32[]{:S(2)}, u32[]{:S(2)}) collective-permute-start(bf16[224,512]{1,0:T(8,128)(2,1)} %get-tuple-element.125), channel_id=1, source_target_pairs={{0,16},{16,0},{1,17},{17,1},{2,18},{18,2},{3,19},{19,3},{4,20},{20... | collective-permute-start | bytes 688136 | tf_op jit(solution)/shard_map/ppermute | solution.py:714
  120.9 8.6 %collective-permute-start.18 = (bf16[224,512]{1,0:T(8,128)(2,1)}, bf16[224,512]{1,0:T(8,128)(2,1)S(1)}, u32[]{:S(2)}, u32[]{:S(2)}) collective-permute-start(bf16[224,512]{1,0:T(8,128)(2,1)} %get-tuple-element.124), channel_id=1, source_target_pairs={{0,1},{1,0},{2,3},{3,2},{4,5},{5,4},{6,7},{7,6},{8,9},{9,8},{10,11... | collective-permute-start | bytes 688136 | tf_op jit(solution)/shard_map/ppermute | solution.py:714
  121.3 11.2 %collective-permute-start.22 = (bf16[224,512]{1,0:T(8,128)(2,1)}, bf16[224,512]{1,0:T(8,128)(2,1)S(1)}, u32[]{:S(2)}, u32[]{:S(2)}) collective-permute-start(bf16[224,512]{1,0:T(8,128)(2,1)} %get-tuple-element.124), channel_id=1, source_target_pairs={{0,16},{16,0},{1,17},{17,1},{2,18},{18,2},{3,19},{19,3},{4,20},{20... | collective-permute-start | bytes 688136 | tf_op jit(solution)/shard_map/ppermute | solution.py:714
  122.0 13.0 %collective-permute-start.26 = (bf16[224,512]{1,0:T(8,128)(2,1)}, bf16[224,512]{1,0:T(8,128)(2,1)S(1)}, u32[]{:S(2)}, u32[]{:S(2)}) collective-permute-start(bf16[224,512]{1,0:T(8,128)(2,1)} %get-tuple-element.125), channel_id=1, source_target_pairs={{0,1},{1,0},{2,3},{3,2},{4,5},{5,4},{6,7},{7,6},{8,9},{9,8},{10,11... | collective-permute-start | bytes 688136 | tf_op jit(solution)/shard_map/ppermute | solution.py:714
  127.5 8.0 %copy-start.6 = (bf16[224,512]{1,0:T(8,128)(2,1)}, bf16[224,512]{1,0:T(8,128)(2,1)S(1)}, u32[]{:S(2)}) copy-start(bf16[224,512]{1,0:T(8,128)(2,1)S(1)} %collective-permute-done.20.refs_1_) | copy-start | bytes 688132
  127.5 12.9 %collective-permute-start.21 = (bf16[224,512]{1,0:T(8,128)(2,1)S(1)}, bf16[224,512]{1,0:T(8,128)(2,1)S(1)}, u32[]{:S(2)}, u32[]{:S(2)}) collective-permute-start(bf16[224,512]{1,0:T(8,128)(2,1)S(1)} %collective-permute-done.20.refs_1_), channel_id=1, source_target_pairs={{0,1},{1,0},{2,3},{3,2},{4,5},{5,4},{6,7},{7,6},{8,9},{9,8},{10,11... | collective-permute-start | bytes 688136 | tf_op jit(solution)/shard_map/ppermute | solution.py:714
  129.5 6.0 %copy-start.7 = (bf16[224,512]{1,0:T(8,128)(2,1)}, bf16[224,512]{1,0:T(8,128)(2,1)S(1)}, u32[]{:S(2)}) copy-start(bf16[224,512]{1,0:T(8,128)(2,1)S(1)} %collective-permute-done.18.refs_2_) | copy-start | bytes 688132
  129.5 11.1 %collective-permute-start.19 = (bf16[224,512]{1,0:T(8,128)(2,1)S(1)}, bf16[224,512]{1,0:T(8,128)(2,1)S(1)}, u32[]{:S(2)}, u32[]{:S(2)}) collective-permute-start(bf16[224,512]{1,0:T(8,128)(2,1)S(1)} %collective-permute-done.18.refs_2_), channel_id=1, source_target_pairs={{0,16},{16,0},{1,17},{17,1},{2,18},{18,2},{3,19},{19,3},{4,20},{20... | collective-permute-start | bytes 688136 | tf_op jit(solution)/shard_map/ppermute | solution.py:714
  132.4 3.1 %copy-start.9 = (bf16[224,512]{1,0:T(8,128)(2,1)}, bf16[224,512]{1,0:T(8,128)(2,1)S(1)}, u32[]{:S(2)}) copy-start(bf16[224,512]{1,0:T(8,128)(2,1)S(1)} %collective-permute-done.22.refs_3_) | copy-start | bytes 688132
  132.4 8.6 %collective-permute-start.23 = (bf16[224,512]{1,0:T(8,128)(2,1)S(1)}, bf16[224,512]{1,0:T(8,128)(2,1)}, u32[]{:S(2)}, u32[]{:S(2)}) collective-permute-start(bf16[224,512]{1,0:T(8,128)(2,1)S(1)} %collective-permute-done.22.refs_3_), channel_id=1, source_target_pairs={{0,8},{8,0},{1,9},{9,1},{2,10},{10,2},{3,11},{11,3},{4,12},{12,4},... | collective-permute-start | bytes 688136 | tf_op jit(solution)/shard_map/ppermute | solution.py:714
  135.0 6.1 %collective-permute-start.25 = (bf16[224,512]{1,0:T(8,128)(2,1)S(1)}, bf16[224,512]{1,0:T(8,128)(2,1)}, u32[]{:S(2)}, u32[]{:S(2)}) collective-permute-start(bf16[224,512]{1,0:T(8,128)(2,1)S(1)} %collective-permute-done.18.refs_2_), channel_id=1, source_target_pairs={{0,8},{8,0},{1,9},{9,1},{2,10},{10,2},{3,11},{11,3},{4,12},{12,4},... | collective-permute-start | bytes 688136 | tf_op jit(solution)/shard_map/ppermute | solution.py:714
  135.5 5.6 %collective-permute-start.27 = (bf16[224,512]{1,0:T(8,128)(2,1)S(1)}, bf16[224,512]{1,0:T(8,128)(2,1)}, u32[]{:S(2)}, u32[]{:S(2)}) collective-permute-start(bf16[224,512]{1,0:T(8,128)(2,1)S(1)} %collective-permute-done.26.refs_4_), channel_id=1, source_target_pairs={{0,8},{8,0},{1,9},{9,1},{2,10},{10,2},{3,11},{11,3},{4,12},{12,4},... | collective-permute-start | bytes 688136 | tf_op jit(solution)/shard_map/ppermute | solution.py:714
  140.4 1.8 %collective-permute-start.24 = (bf16[224,512]{1,0:T(8,128)(2,1)}, bf16[224,512]{1,0:T(8,128)(2,1)S(1)}, u32[]{:S(2)}, u32[]{:S(2)}) collective-permute-start(bf16[224,512]{1,0:T(8,128)(2,1)} %copy-done.6), channel_id=1, source_target_pairs={{0,8},{8,0},{1,9},{9,1},{2,10},{10,2},{3,11},{11,3},{4,12},{12,4},... | collective-permute-start | bytes 688136 | tf_op jit(solution)/shard_map/ppermute | solution.py:714
  140.6 1.7 %collective-permute-start.29 = (bf16[224,512]{1,0:T(8,128)(2,1)S(1)}, bf16[224,512]{1,0:T(8,128)(2,1)S(1)}, u32[]{:S(2)}, u32[]{:S(2)}) collective-permute-start(bf16[224,512]{1,0:T(8,128)(2,1)S(1)} %collective-permute-done.19.refs_0_), channel_id=1, source_target_pairs={{0,8},{8,0},{1,9},{9,1},{2,10},{10,2},{3,11},{11,3},{4,12},{12,4},... | collective-permute-start | bytes 688136 | tf_op jit(solution)/shard_map/ppermute | solution.py:714
  141.0 1.6 %collective-permute-start.30 = (bf16[224,512]{1,0:T(8,128)(2,1)S(1)}, bf16[224,512]{1,0:T(8,128)(2,1)S(1)}, u32[]{:S(2)}, u32[]{:S(2)}) collective-permute-start(bf16[224,512]{1,0:T(8,128)(2,1)S(1)} %collective-permute-done.21.refs_1_), channel_id=1, source_target_pairs={{0,8},{8,0},{1,9},{9,1},{2,10},{10,2},{3,11},{11,3},{4,12},{12,4},... | collective-permute-start | bytes 688136 | tf_op jit(solution)/shard_map/ppermute | solution.py:714
  (19 other events, 21.5 us)
